TPU v7x, 256 devices: a whole 4x4x8 slice. The times are simulated.
256 devices in a mesh: dp: 32 (over x, z), head: 8 (over y, core).
Axes of the slice: x: 4, y: 4, z: 8, core: 2. Of those that a mesh axis runs over, the one named last changes fastest.
Arguments:
- key_grads: bfloat16 [2, 16384, 2048], P(None, 'dp', 'head'), may hold values from -6 to 6
- value_grads: bfloat16 [2, 16384, 2048], P(None, 'dp', 'head'), may hold values from -6 to 6
- key_weight: bfloat16 [2, 3584, 2048], P(None, 'dp', 'head'), may hold values from -0.125 to 0.125
- value_weight: bfloat16 [2, 3584, 2048], P(None, 'dp', 'head'), may hold values from -0.125 to 0.125
- block_source: int32 [1024], replicated, may hold values from 0 to 1023, as said below
- hidden_mid: bfloat16 [16384, 3584], P('dp', 'head')
- mlp_out: bfloat16 [16384, 3584], P('dp', 'head')
- post_gain: bfloat16 [3584], P('head'), may hold values from 0.5 to 2
- final_gain: bfloat16 [3584], P('head'), may hold values from 0.5 to 2
- gate_pre: bfloat16 [16384, 7168], P('dp', 'head'), may hold values from -6 to 6
- up_pre: bfloat16 [16384, 7168], P('dp', 'head'), may hold values from -6 to 6
- down_weight: bfloat16 [7168, 3584], P('head', 'dp'), may hold values from -0.09375 to 0.09375
Outputs:
- resid_grad: bfloat16 [16384, 3584], P('dp', 'head')
- gate_grad: bfloat16 [16384, 7168], P('dp', 'head')
- up_grad: bfloat16 [16384, 7168], P('dp', 'head')
Inputs may be any that keep to these rules, and one draw needn't show every extreme that they name: block_source is a permutation of the 1024 row blocks. The decoder blocks of one device are blocks 32 * a to 32 * a + 31, and the encoder blocks of device b are blocks 32 * b to 32 * b + 31; at most 2 decoder blocks of one device fill encoder blocks of one device, and exactly 2 do for some pairs of devices in every draw.
All inputs are finite; a program needn't handle non-finite values.
Results may differ from a plain program's by a relative error of at most 0.02.
Values may be sent and summed in bfloat16 or wider, within the bound.
No kernel may reach another device: no remote copies, remote signals or barrier semaphores. Data moves between devices by JAX's collectives and lax.ppermute only.
A program may use at most 64 MiB of HBM per device.

v0:
```python
import jax
import jax.numpy as jnp
from jax import lax
from jax.sharding import PartitionSpec as P

CAP = 2


epsilon = 1e-06


def gelu_parts(gate_value):
    activated, pullback = jax.vjp(
        lambda pre_act: jax.nn.gelu(pre_act, approximate=True), gate_value
    )
    return (activated, pullback(jnp.ones_like(gate_value))[0])


def repack(dec_memory, block_source, dev_blocks):
    row_count, col_share = dec_memory.shape
    block_rows = row_count // dev_blocks
    total_blocks = dev_blocks * dev_blocks
    slot_count = dev_blocks * CAP
    this_dev = lax.axis_index("dp")
    block_ids = jnp.arange(total_blocks, dtype=jnp.int32)
    is_source = block_source[:, None] == block_ids[None, :]
    dest_block = jnp.sum(jnp.where(is_source, block_ids[:, None], 0), axis=0)
    dest_device = (dest_block // dev_blocks).reshape(dev_blocks, dev_blocks)
    same_dest = dest_device[:, :, None] == dest_device[:, None, :]
    slot_ids = jnp.arange(dev_blocks, dtype=jnp.int32)
    before_slot = slot_ids[None, :] < slot_ids[:, None]
    dest_rank = jnp.sum((same_dest & before_slot[None, :, :]).astype(jnp.int32), axis=2)
    own_dest = lax.dynamic_index_in_dim(dest_device, this_dev, 0, keepdims=False)
    own_rank = lax.dynamic_index_in_dim(dest_rank, this_dev, 0, keepdims=False)
    send_slot = own_dest * CAP + own_rank
    buffer_ids = jnp.arange(slot_count, dtype=jnp.int32)
    send_pick = (buffer_ids[:, None] == send_slot[None, :]).astype(jnp.bfloat16)
    local_rows = dec_memory.reshape(dev_blocks, block_rows * col_share)
    outgoing = jnp.dot(send_pick, local_rows, preferred_element_type=jnp.float32).astype(
        jnp.bfloat16
    )
    outgoing = outgoing.reshape(dev_blocks, CAP * block_rows, col_share)
    incoming = lax.all_to_all(outgoing, "dp", split_axis=0, concat_axis=0, tiled=True)
    own_sources = lax.dynamic_slice_in_dim(block_source, this_dev * dev_blocks, dev_blocks)
    source_device = own_sources // dev_blocks
    flat_ranks = dest_rank.reshape(-1)
    source_rank = jnp.sum(
        jnp.where(block_ids[None, :] == own_sources[:, None], flat_ranks[None, :], 0), axis=1
    )
    recv_slot = source_device * CAP + source_rank
    recv_pick = (recv_slot[:, None] == buffer_ids[None, :]).astype(jnp.bfloat16)
    arrived = incoming.reshape(slot_count, block_rows * col_share)
    placed = jnp.dot(recv_pick, arrived, preferred_element_type=jnp.float32).astype(jnp.bfloat16)
    return placed.reshape(row_count, col_share)


def per_device(
    key_grads,
    value_grads,
    key_weight,
    value_weight,
    block_source,
    hidden_mid,
    mlp_out,
    post_gain,
    final_gain,
    gate_pre,
    up_pre,
    down_weight,
):
    row_count, col_share = hidden_mid.shape
    width = col_share * lax.axis_size("head")
    dev_blocks = lax.axis_size("dp")
    key_piece = lax.all_gather(key_weight, "dp", axis=1, tiled=True)
    value_piece = lax.all_gather(value_weight, "dp", axis=1, tiled=True)
    term = jnp.einsum("lrk,lck->rc", key_grads, key_piece, preferred_element_type=jnp.float32)
    term = term + jnp.einsum(
        "lrk,lck->rc", value_grads, value_piece, preferred_element_type=jnp.float32
    )
    dec_memory = lax.psum_scatter(
        term.astype(jnp.bfloat16), "head", scatter_dimension=1, tiled=True
    )
    memory_grad = repack(dec_memory, block_source, dev_blocks)
    mid_value = hidden_mid.astype(jnp.float32)
    out_value = mlp_out.astype(jnp.float32)
    gain_post = post_gain.astype(jnp.float32)
    gain_final = final_gain.astype(jnp.float32)
    sum_out = lax.psum(jnp.sum(out_value * out_value, axis=1), "head")
    out_scale = lax.rsqrt(sum_out / width + epsilon)[:, None]
    resid = mid_value + out_value * out_scale * gain_post
    sum_resid = lax.psum(jnp.sum(resid * resid, axis=1), "head")
    resid_scale = lax.rsqrt(sum_resid / width + epsilon)[:, None]
    norm_grad = memory_grad.astype(jnp.float32) * gain_final
    final_dot = lax.psum(jnp.sum(norm_grad * resid, axis=1), "head")
    final_mean = resid_scale * final_dot[:, None] / width
    resid_total = resid_scale * (norm_grad - resid * resid_scale * final_mean)
    post_input = resid_total * gain_post
    post_dot = lax.psum(jnp.sum(post_input * out_value, axis=1), "head")
    post_mean = out_scale * post_dot[:, None] / width
    post_grad = out_scale * (post_input - out_value * out_scale * post_mean)
    post_full = lax.all_gather(post_grad.astype(jnp.bfloat16), "head", axis=1, tiled=True)
    hidden_grad = lax.dot_general(
        post_full,
        lax.all_gather(down_weight, "dp", axis=1, tiled=True),
        (((1,), (1,)), ((), ())),
        preferred_element_type=jnp.float32,
    )
    activated, slope = gelu_parts(gate_pre.astype(jnp.float32))
    gate_grad = (hidden_grad * up_pre.astype(jnp.float32) * slope).astype(jnp.bfloat16)
    up_grad = (hidden_grad * activated).astype(jnp.bfloat16)
    return (resid_total.astype(jnp.bfloat16), gate_grad, up_grad)


def solution(mesh):
    return jax.shard_map(
        per_device,
        mesh=mesh,
        in_specs=(
            P(None, "dp", "head"),
            P(None, "dp", "head"),
            P(None, "dp", "head"),
            P(None, "dp", "head"),
            P(),
            P("dp", "head"),
            P("dp", "head"),
            P("head"),
            P("head"),
            P("dp", "head"),
            P("dp", "head"),
            P("head", "dp"),
        ),
        out_specs=(P("dp", "head"), P("dp", "head"), P("dp", "head")),
        check_vma=False,
    )
```

profile of v0, /device:TPU:33, one launch (start us, length us, event | category | flops | bytes accessed | tf_op | source)
XLA Modules:
  0.0 364.8 jit_solution(18254989760330669023)
XLA Ops:
  7.2 0.0 copy-start
  7.2 0.0 all-gather.5.cloned.1.call-start
  7.2 0.7 all-gather.5.cloned.1.call-update
  7.9 0.0 all-gather.7.cloned.1.call-start
  8.0 0.7 all-gather.7.cloned.1.call-update
  8.7 0.0 reduce-scatter.2.cloned.1.call-start
  8.7 81.8 %all-gather.5.cloned.1.call-done = bf16[2,3584,256]{2,1,0:T(8,128)(2,1)} async-done(((bf16[2,112,256]{2,1,0:T(8,128)(2,1)}), bf16[2,3584,256]{2,1,0:T(8,128)(2,1)}) %all-gather.5.cloned.1.call-update) | async-done | bytes 3670032 | tf_op jit(solution)/shard_map/all_gather | solution.py:74
  90.5 7.1 %fusion.25 = f32[512,3584,1]{0,1,2:T(8,128)} fusion(bf16[2,512,256]{2,1,0:T(8,128)(2,1)S(1)} %copy-done, bf16[2,3584,256]{2,1,0:T(8,128)(2,1)} %all-gather.5.cloned.1.call-done), kind=kOutput, calls=%fused_computation.62 | convolution fusion | flops 1879048192 | bytes 11534336 | tf_op jit(solution)/shard_map/lrk,lck->rc/dot_general | solution.py:76
  97.6 73.3 %all-gather.7.cloned.1.call-done = bf16[2,3584,256]{2,1,0:T(8,128)(2,1)} async-done(((bf16[2,112,256]{2,1,0:T(8,128)(2,1)}), bf16[2,3584,256]{2,1,0:T(8,128)(2,1)}) %all-gather.7.cloned.1.call-update) | async-done | bytes 3670032 | tf_op jit(solution)/shard_map/all_gather | solution.py:75
  170.9 8.2 %fusion.1 = bf16[512,3584]{0,1:T(8,128)(2,1)} fusion(f32[512,3584,1]{0,1,2:T(8,128)} %fusion.25, bf16[2,512,256]{2,1,0:T(8,128)(2,1)S(1)} %copy-done.1, bf16[2,3584,256]{2,1,0:T(8,128)(2,1)} %all-gather.7.cloned.1.call-done), kind=kOutput, calls=%fused_computation.4 | convolution fusion | flops 1882718208 | bytes 15204352 | tf_op jit(solution)/shard_map/lrk,lck->rc/dot_general | solution.py:77
  179.1 0.0 reduce-scatter.2.cloned.1.call-update
  179.1 0.0 all-gather.11.cloned.1.call-start
  179.2 0.5 all-gather.11.cloned.1.call-update
  179.7 0.1 copy-done.6
  179.8 0.5 select_reduce_fusion
  180.3 0.1 reduce_sum.68
  180.4 0.8 convert_reduce_fusion
  181.2 35.0 %reduce-scatter.2.cloned.1.call-done = bf16[512,448]{0,1:T(8,128)(2,1)} async-done(((bf16[512,3584]{0,1:T(8,128)(2,1)}), bf16[512,448]{0,1:T(8,128)(2,1)}) %reduce-scatter.2.cloned.1.call-update) | async-done | bytes 458768 | tf_op jit(solution)/shard_map/reduce_scatter | solution.py:80
  216.2 1.2 copy.27
  217.4 0.6 reshape.102
  218.0 0.4 convolution_convert_fusion
  218.4 2.3 reshape.103
  220.6 9.7 %all-to-all-start = ((bf16[32,32,448]{2,1,0:T(8,128)(2,1)}), bf16[32,32,448]{2,1,0:T(8,128)(2,1)S(1)}, u32[]{:S(2)}, u32[]{:S(2)}) async-start(bf16[32,32,448]{2,1,0:T(8,128)(2,1)} %reshape.103), calls=%async_computation.1 | async-start | bytes 2097152 | tf_op jit(solution)/shard_map/all_to_all | solution.py:43
  230.3 0.0 all-gather.9.cloned.1.call-start
  230.4 0.7 broadcast_in_dim.28
  231.1 1.3 dynamic_slice.10
  232.4 0.2 copy.26
  232.6 0.2 copy.25
  232.8 0.7 convert_element_type.59
  233.5 0.2 fusion.19
  233.7 16.3 %psum.28 = f32[512]{0:T(512)S(1)} all-reduce(f32[512]{0:T(512)S(1)} %fusion.19), channel_id=1, replica_groups=mesh['dp'=32,'head'=8] {'head'}, use_global_device_ids=true, to_apply=%region_1.2 | all-reduce | flops 512 | bytes 4096 | tf_op jit(solution)/shard_map/psum | solution.py:88
  249.9 0.8 select_reduce_fusion.1
  250.8 1.3 multiply_add_fusion
  252.1 7.4 %all-to-all-done = bf16[32,32,448]{2,1,0:T(8,128)(2,1)S(1)} async-done(((bf16[32,32,448]{2,1,0:T(8,128)(2,1)}), bf16[32,32,448]{2,1,0:T(8,128)(2,1)S(1)}, u32[]{:S(2)}, u32[]{:S(2)}) %all-to-all-start) | async-done | bytes 917536 | tf_op jit(solution)/shard_map/all_to_all | solution.py:43
  259.5 1.2 reshape.104
  260.7 1.9 fusion
  262.6 1.7 reshape.105
  264.3 0.6 multiply_reduce_fusion.1
  264.9 18.9 %all-reduce = (f32[512]{0:T(512)S(1)}, f32[512]{0:T(512)S(1)}) all-reduce(f32[512]{0:T(512)S(1)} %get-tuple-element.13, f32[512]{0:T(512)S(1)} %get-tuple-element.12), channel_id=1, replica_groups=mesh['dp'=32,'head'=8] {'head'}, use_global_device_ids=true, to_apply=%region_9.10 | all-reduce | flops 1024 | bytes 8192 | tf_op jit(solution)/shard_map/psum | solution.py:94
  283.8 1.7 fusion.20
  285.5 16.1 %psum.31 = f32[512]{0:T(512)S(1)} all-reduce(f32[512]{0:T(512)S(1)} %get-tuple-element.16), channel_id=1, replica_groups=mesh['dp'=32,'head'=8] {'head'}, use_global_device_ids=true, to_apply=%region_11.12 | all-reduce | flops 512 | bytes 4096 | tf_op jit(solution)/shard_map/psum | solution.py:98
  301.6 1.9 fusion.18
  303.5 1.0 copy.28
  304.4 0.0 all-gather.9.cloned.1.call-update
  304.5 1.0 copy.29
  305.4 8.1 %all-gather.11.cloned.1.call-done = bf16[896,3584]{0,1:T(8,128)(2,1)} async-done(((bf16[896,112]{0,1:T(8,128)(2,1)}), bf16[896,3584]{0,1:T(8,128)(2,1)}) %all-gather.11.cloned.1.call-update) | async-done | bytes 6422544 | tf_op jit(solution)/shard_map/all_gather | solution.py:104
  313.6 34.2 %all-gather.9.cloned.1.call-done = bf16[512,3584]{0,1:T(8,128)(2,1)} async-done(((bf16[512,448]{0,1:T(8,128)(2,1)}), bf16[512,3584]{0,1:T(8,128)(2,1)}) %all-gather.9.cloned.1.call-update) | async-done | bytes 3670032 | tf_op jit(solution)/shard_map/all_gather | solution.py:101
  347.8 10.4 %fusion.12 = (bf16[512,896]{1,0:T(8,128)(2,1)}, bf16[512,896]{1,0:T(8,128)(2,1)}) fusion(bf16[512,896]{1,0:T(8,128)(2,1)S(1)} %copy-done.7, bf16[512,896]{1,0:T(8,128)(2,1)} %param.22, bf16[512,3584]{0,1:T(8,128)(2,1)} %all-gather.9.cloned.1.call-done, bf16[896,3584]{0,1:T(8,128)(2,1)} %all-gather.11.cloned.1.call-done), kind=kOutput, calls=%fused_computation.22 | convolution fusion | flops 3299803136 | bytes 13762560 | tf_op jit(solution)/shard_map/dot_general | solution.py:102
  (21 shorter events, 0.1 us)
Async XLA Ops:
  7.2 83.3 %copy-start = (bf16[2,512,256]{2,1,0:T(8,128)(2,1)S(1)}, bf16[2,512,256]{2,1,0:T(8,128)(2,1)}, u32[]{:S(2)}) copy-start(bf16[2,512,256]{2,1,0:T(8,128)(2,1)} %param.12) | copy-start | bytes 1572868
  7.2 83.3 %all-gather.5.cloned.1.call-start = ((), (), s32[]{:S(2)}) async-start(), calls=%async_computation.2 | async-start | bytes 3784704 | tf_op jit(solution)/shard_map/all_gather | solution.py:74
  7.9 163.0 %all-gather.7.cloned.1.call-start = ((), (), s32[]{:S(2)}) async-start(), calls=%async_computation.3 | async-start | bytes 3784704 | tf_op jit(solution)/shard_map/all_gather | solution.py:75
  8.7 162.2 %copy-start.1 = (bf16[2,512,256]{2,1,0:T(8,128)(2,1)S(1)}, bf16[2,512,256]{2,1,0:T(8,128)(2,1)}, u32[]{:S(2)}) copy-start(bf16[2,512,256]{2,1,0:T(8,128)(2,1)} %param.13) | copy-start | bytes 1572868
  8.7 207.5 %reduce-scatter.2.cloned.1.call-start = ((), (), s32[]{:S(2)}) async-start(), calls=%async_computation.4 | async-start | bytes 4128768 | tf_op jit(solution)/shard_map/reduce_scatter | solution.py:80
  179.1 0.7 copy-start.6
  179.1 134.5 %all-gather.11.cloned.1.call-start = ((), (), s32[]{:S(2)}) async-start(), calls=%async_computation.6 | async-start | bytes 6623232 | tf_op jit(solution)/shard_map/all_gather | solution.py:104
  218.4 14.0 %copy-start.2 = (bf16[512,448]{0,1:T(8,128)(2,1)S(1)}, bf16[512,448]{0,1:T(8,128)(2,1)}, u32[]{:S(2)}) copy-start(bf16[512,448]{0,1:T(8,128)(2,1)} %param.18) | copy-start | bytes 1376260
  220.6 11.9 %copy-start.5 = (bf16[448]{0:T(512)(128)(2,1)S(1)}, bf16[448]{0:T(512)(128)(2,1)}, u32[]{:S(2)}) copy-start(bf16[448]{0:T(512)(128)(2,1)} %param.19) | copy-start | bytes 2692
  220.6 11.9 %copy-start.3 = (bf16[512,448]{0,1:T(8,128)(2,1)S(1)}, bf16[512,448]{0,1:T(8,128)(2,1)}, u32[]{:S(2)}) copy-start(bf16[512,448]{0,1:T(8,128)(2,1)} %param.17) | copy-start | bytes 1376260
  220.6 38.9 %all-to-all-start = ((bf16[32,32,448]{2,1,0:T(8,128)(2,1)}), bf16[32,32,448]{2,1,0:T(8,128)(2,1)S(1)}, u32[]{:S(2)}, u32[]{:S(2)}) async-start(bf16[32,32,448]{2,1,0:T(8,128)(2,1)} %reshape.103), calls=%async_computation.1 | async-start | bytes 2097152 | tf_op jit(solution)/shard_map/all_to_all | solution.py:43
  230.3 117.5 %all-gather.9.cloned.1.call-start = ((), (), s32[]{:S(2)}) async-start(), calls=%async_computation.5 | async-start | bytes 4128768 | tf_op jit(solution)/shard_map/all_gather | solution.py:101
  231.1 18.9 %copy-start.4 = (s32[1024]{0:T(1024)S(1)}, s32[1024]{0:T(1024)}, u32[]{:S(2)}) copy-start(s32[1024]{0:T(1024)} %broadcast_in_dim.28) | copy-start | bytes 12292
  303.5 44.4 %copy-start.7 = (bf16[512,896]{1,0:T(8,128)(2,1)S(1)}, bf16[512,896]{1,0:T(8,128)(2,1)}, u32[]{:S(2)}) copy-start(bf16[512,896]{1,0:T(8,128)(2,1)} %param.21) | copy-start | bytes 2752516
Sparse Core Ops, SparseCore 0:
  10.6 79.8 all-gather.4
  93.1 77.7 all-gather.6
  179.2 36.9 reduce-scatter.1
  218.6 94.8 all-gather.10
  315.8 31.9 all-gather.8
where the time goes:
time: 366 us; the launch traced here: 365 us
  waiting for transfers between devices  242 us (66%)
  blocking collectives  51.2 us (14%)
  matrix products  28 us (8%)
  between operations  13.9 us (4%)
  local copies, waits for them, and re-layouts  11.4 us (3%)
  starting transfers between devices  9.9 us (3%)
  other arithmetic  8.52 us (2%)
    all_gather x1, waiting for transfers between devices, per_device(): key_piece = lax.all_gather(key_weight, 'dp', axis=1, tiled=True)  81.8 us
    all_gather x1, waiting for transfers between devices, per_device(): value_piece = lax.all_gather(value_weight, 'dp', axis=1, tiled=True)  73.3 us
    reduce_scatter x1, waiting for transfers between devices, per_device(): lax.psum_scatter(term.astype(jnp.bfloat16), 'head', scatter_dimension=1,...  35 us
    all_gather x1, waiting for transfers between devices, per_device(): lax.all_gather(post_grad.astype(jnp.bfloat16), 'head', axis=1, tiled=True)  34.2 us
    psum x1, blocking collectives, per_device(): final_dot = lax.psum(jnp.sum(norm_grad * resid, axis=1), 'head')  18.9 us
    psum x1, blocking collectives, per_device(): sum_out = lax.psum(jnp.sum(out_value * out_value, axis=1), 'head')  16.3 us
    psum x1, blocking collectives, per_device(): post_dot = lax.psum(jnp.sum(post_input * out_value, axis=1), 'head')  16.1 us
    dot_general x1, matrix products, per_device(): lax.dot_general(post_full, lax.all_gather(down_weight, 'dp', axis=1, tile...  10.4 us
  transfers between devices with their start and end apart: 6, of which 6 were waited for; matrix products, arithmetic and copies ran while one was open for 8% of the time, Pallas kernels for 0%

commit v1 on v0

v1 whole, which is shorter than its diff:
```python
import jax
import jax.numpy as jnp
from jax import lax
from jax.experimental import pallas as pl
from jax.experimental.pallas import tpu as pltpu
from jax.sharding import PartitionSpec as P

EPS = 1e-06
NX, NZ, NY, NC = 4, 8, 4, 2
AXES = ("dp", "head")
BF = jnp.bfloat16
F32 = jnp.float32
VMEM_LIMIT = 56 * 1024 * 1024


def move(value, dx=0, dz=0, dy=0, dc=0):
    pairs = []
    for x in range(NX):
        for z in range(NZ):
            for y in range(NY):
                for c in range(NC):
                    src = (x * NZ + z) * 8 + y * NC + c
                    dst = (
                        ((x + dx) % NX * NZ + (z + dz) % NZ) * 8
                        + (y + dy) % NY * NC
                        + (c + dc) % NC
                    )
                    pairs.append((src, dst))
    return lax.ppermute(value, AXES, pairs)


def spread_columns(shard):
    pairs = []
    for x in range(NX):
        for z in range(NZ):
            for head in range(8):
                c, t = z // 4, z % 4
                pairs.append(((x * NZ + z) * 8 + head, (t * NZ + 4 * c + x) * 8 + head))
    return lax.ppermute(shard, AXES, pairs)


def call(kernel, out_shape, n_scalar, n_array, flops, scratch=(), name=None):
    return pl.pallas_call(
        kernel,
        out_shape=out_shape,
        in_specs=[pl.BlockSpec(memory_space=pltpu.SMEM)] * n_scalar
        + [pl.BlockSpec(memory_space=pltpu.VMEM)] * n_array,
        out_specs=jax.tree.map(lambda _: pl.BlockSpec(memory_space=pltpu.VMEM), out_shape),
        scratch_shapes=scratch,
        compiler_params=pltpu.CompilerParams(vmem_limit_bytes=VMEM_LIMIT),
        cost_estimate=pl.CostEstimate(flops=flops, bytes_accessed=6_000_000, transcendentals=0),
        name=name,
    )


def dot_nt(a, b):
    return lax.dot_general(a, b, (((1,), (1,)), ((), ())), preferred_element_type=F32)


def dot_tn(a, b):
    return lax.dot_general(a, b, (((0,), (0,)), ((), ())), preferred_element_type=F32)


def part_kernel(slot, w0, f1, f2, f3, g1, g2, g3, oa, ob, r0, r1, r2, r3a, r3b, out, wall):
    for k, ref in enumerate((w0, f1, f2, f3, g1, g2, g3)):
        wall[k * 112 : (k + 1) * 112, :] = ref[...]
    wall[784:848, :] = oa[...]
    wall[848:896, :] = ob[...]
    at = 0
    for ref in (r0, r1, r2, r3a, r3b):
        size = ref.shape[0]
        prod = dot_nt(wall[...], ref[...]).astype(BF)
        for k in range(8):
            out[slot[k], :, at : at + size] = prod[k * 112 : (k + 1) * 112, :]
        at += size


def send_kernel(xs, parts, lane_pos, out, moved):
    for r in range(4):
        total = parts[0, :, r * 512 : (r + 1) * 512].astype(F32)
        for g in range(1, 8):
            total = total + parts[g, :, r * 512 : (r + 1) * 512].astype(F32)
        ids = lax.broadcasted_iota(jnp.int32, (1024, 512), 0)
        pick = jnp.where(ids == lane_pos[r : r + 1, :], 1.0, 0.0).astype(BF)
        moved[xs[r]] = dot_nt(total.astype(BF), pick).astype(BF)
    group = lax.broadcasted_iota(jnp.int32, (112, 128), 1) // 32
    for q in range(8):
        tiles = [moved[x, :, q * 128 : (q + 1) * 128] for x in range(4)]
        for j in range(4):
            here = tiles[(0 - j) % 4]
            for g in range(1, 4):
                here = jnp.where(group == g, tiles[(g - j) % 4], here)
            out[4 * q + j] = here


def recv_kernel(arrived, row_pos, resid, gout, gain_final, grad, dots):
    ids = lax.broadcasted_iota(jnp.int32, (1024, 512), 0)
    pick = jnp.where(ids == row_pos[...], 1.0, 0.0).astype(BF)
    first = jnp.zeros((1, 512), F32)
    second = jnp.zeros((1, 512), F32)
    for x in range(4):
        side = jnp.concatenate([arrived[x * 8 + z] for z in range(8)], axis=1)
        rows = pl.ds(x * 112, 112)
        piece = jnp.dot(side, pick, preferred_element_type=F32)
        piece = piece * gain_final[rows, :]
        grad[rows, :] = piece
        first = first + jnp.sum(piece * resid[rows, :], axis=0, keepdims=True)
        second = second + jnp.sum(piece * gout[rows, :], axis=0, keepdims=True)
    dots[0:1, :] = first
    dots[1:2, :] = second


def norm_kernel(norm_grad, resid, out_value, gain_post, stats, dots, resid_grad, post_grad):
    width = 3584.0
    out_scale = stats[0:1, :]
    resid_scale = stats[1:2, :]
    cross = stats[2:3, :]
    both = dots[0]
    for k in range(1, 8):
        both = both + dots[k]
    final_mean = resid_scale * both[0:1, :] / width
    post_dot = resid_scale * (both[1:2, :] - resid_scale * final_mean * cross)
    post_mean = out_scale * post_dot / width
    total = resid_scale * (norm_grad[...] - resid[...] * (resid_scale * final_mean))
    post = out_scale * (total * gain_post[...] - out_value[...] * (out_scale * post_mean))
    post_grad[...] = post.astype(BF)
    resid_grad[...] = total.T.astype(BF)


def final_kernel(heads, p0, p1, p2, p3, p4, p5, p6, p7, weight, slope, active, gate, up):
    total = jnp.zeros((512, 896), F32)
    for k, ref in enumerate((p0, p1, p2, p3, p4, p5, p6, p7)):
        rows = pl.ds(pl.multiple_of(heads[k] * 448, 64), 448)
        total = total + dot_tn(ref[...], weight[rows, :])
    gate[...] = (total * slope[...]).astype(BF)
    up[...] = (total * active[...]).astype(BF)


def gelu_parts(gate_value):
    activated, pullback = jax.vjp(
        lambda pre_act: jax.nn.gelu(pre_act, approximate=True), gate_value
    )
    return (activated, pullback(jnp.ones_like(gate_value))[0])


def swap_rows(value):
    return lax.all_to_all(
        jnp.broadcast_to(value[None], (8,) + value.shape), "head", 0, 0, tiled=True
    )


def per_device(
    key_grads,
    value_grads,
    key_weight,
    value_weight,
    block_source,
    hidden_mid,
    mlp_out,
    post_gain,
    final_gain,
    gate_pre,
    up_pre,
    down_weight,
):
    dev = lax.axis_index("dp")
    head = lax.axis_index("head")
    x, z = dev // NZ, dev % NZ
    y, c = head // NC, head % NC

    weight = jnp.concatenate([key_weight[0], key_weight[1], value_weight[0], value_weight[1]], 1)
    rows = jnp.concatenate([key_grads[0], key_grads[1], value_grads[0], value_grads[1]], 1)
    r1 = move(rows, dx=1)
    r2 = move(rows, dx=-1)
    w0 = spread_columns(weight)
    f1, g1 = move(w0, dz=1), move(w0, dz=-1)
    f2, g2 = move(f1, dz=1), move(g1, dz=-1)
    f3, g3 = move(f2, dz=1), move(g2, dz=-1)
    oa, ob = move(f3[:64], dz=1), move(g3[64:], dz=-1)
    r3a = move(r1[:256], dx=1)
    r3b = move(r2[256:], dx=-1)

    block_ids = jnp.arange(1024, dtype=jnp.int32)
    is_source = block_source[:, None] == block_ids[None, :]
    dest_block = jnp.sum(jnp.where(is_source, block_ids[:, None], 0), axis=0)
    dest_device = (dest_block // 32).reshape(32, 32)
    same_dest = dest_device[:, :, None] == dest_device[:, None, :]
    slot_ids = jnp.arange(32, dtype=jnp.int32)
    before = slot_ids[None, :] < slot_ids[:, None]
    rank = jnp.sum((same_dest & before[None]).astype(jnp.int32), axis=2)
    own_x = jnp.stack([x, (x + 3) % 4, (x + 1) % 4, (x + 2) % 4]).astype(jnp.int32)
    dest_own = dest_device[own_x * NZ + z]
    rank_own = rank[own_x * NZ + z]
    lanes = (
        (dest_own // 4) * 128 + ((dest_own % 4 + own_x[:, None]) % 4) * 32 + rank_own * 16
    )
    lane_pos = (lanes[:, :, None] + jnp.arange(16, dtype=jnp.int32)).reshape(4, 512)
    source = lax.dynamic_slice_in_dim(block_source, dev * 32, 32)
    source_dev = source // 32
    source_rank = jnp.sum(
        jnp.where(block_ids[None, :] == source[:, None], rank.reshape(-1)[None, :], 0), axis=1
    )
    spot = (
        (source_dev % NZ) * 128 + ((dev % 4 + source_dev // NZ) % 4) * 32 + source_rank * 16
    )
    row_pos = (spot[:, None] + jnp.arange(16, dtype=jnp.int32)).reshape(1, 512)

    gain_post = post_gain.astype(F32)[:, None]
    gain_final = final_gain.astype(F32)[:, None]
    out_value = mlp_out.T.astype(F32)
    mid_value = hidden_mid.T.astype(F32)
    sum_out = jnp.sum(swap_rows(jnp.sum(out_value * out_value, axis=0)[None]), axis=0)
    out_scale = lax.rsqrt(sum_out / 3584 + EPS)
    gout = out_value * gain_post
    resid = mid_value + gout * out_scale
    pair = jnp.stack([jnp.sum(resid * resid, axis=0), jnp.sum(resid * gout, axis=0)])
    pair = jnp.sum(swap_rows(pair), axis=0)
    resid_scale = lax.rsqrt(pair[0:1] / 3584 + EPS)
    stats = jnp.concatenate([out_scale, resid_scale, pair[1:2]], axis=0)
    active, slope = gelu_parts(gate_pre.astype(F32))
    slope = slope * up_pre.astype(F32)
    down = lax.all_gather(down_weight.T, "dp", axis=0, tiled=True)

    pos = (z - jnp.array([0, 1, 2, 3, -1, -2, -3, 4], jnp.int32)) % NZ
    slot = (2 * (pos % 4) + pos // 4).astype(jnp.int32)
    parts = call(
        part_kernel,
        jax.ShapeDtypeStruct((8, 112, 2048), BF),
        1,
        14,
        2 * 2048 * 896 * 1024,
        [pltpu.VMEM((896, 1024), BF)],
        name="part",
    )(slot, w0, f1, f2, f3, g1, g2, g3, oa, ob, rows, r1, r2, r3a, r3b)
    parts = lax.all_to_all(parts, "head", 0, 0, tiled=True)
    outgoing = call(
        send_kernel,
        jax.ShapeDtypeStruct((32, 112, 128), BF),
        1,
        2,
        2 * 112 * 2048 * 1024,
        [pltpu.VMEM((4, 112, 1024), BF)],
        name="send",
    )(own_x, parts, lane_pos)
    arrived = lax.all_to_all(outgoing, "dp", 0, 0, tiled=True)
    norm_grad, dots = call(
        recv_kernel,
        (jax.ShapeDtypeStruct((448, 512), F32), jax.ShapeDtypeStruct((2, 512), F32)),
        0,
        5,
        2 * 448 * 512 * 1024,
        name="recv",
    )(arrived, row_pos, resid, gout, gain_final)
    dots = swap_rows(dots)
    resid_grad, post = call(
        norm_kernel,
        (jax.ShapeDtypeStruct((512, 448), BF), jax.ShapeDtypeStruct((448, 512), BF)),
        0,
        6,
        448 * 512 * 20,
        name="norm",
    )(norm_grad, resid, out_value, gain_post, stats, dots)
    s0 = move(post, dc=1)
    p1, p2, p3 = move(post, dy=1), move(post, dy=-1), move(post, dy=2)
    s1, s2, s3 = move(p1, dc=1), move(p2, dc=1), move(p3, dc=1)
    from_y = jnp.stack([y, y, y + 3, y + 3, y + 1, y + 1, y + 2, y + 2]) % 4
    from_c = (c + jnp.array([0, 1] * 4, jnp.int32)) % 2
    heads = (from_y * 2 + from_c).astype(jnp.int32)
    gate_grad, up_grad = call(
        final_kernel,
        (jax.ShapeDtypeStruct((512, 896), BF), jax.ShapeDtypeStruct((512, 896), BF)),
        1,
        11,
        2 * 512 * 896 * 3584,
        name="final",
    )(heads, post, s0, p1, s1, p2, s2, p3, s3, down, slope, active)
    return (resid_grad, gate_grad, up_grad)


def solution(mesh):
    return jax.shard_map(
        per_device,
        mesh=mesh,
        in_specs=(
            P(None, "dp", "head"),
            P(None, "dp", "head"),
            P(None, "dp", "head"),
            P(None, "dp", "head"),
            P(),
            P("dp", "head"),
            P("dp", "head"),
            P("head"),
            P("head"),
            P("dp", "head"),
            P("dp", "head"),
            P("head", "dp"),
        ),
        out_specs=(P("dp", "head"), P("dp", "head"), P("dp", "head")),
        check_vma=False,
    )
```

time: 366 us -> 247 us (0.67)
  waiting for transfers between devices: 242 us -> 104 us
  starting transfers between devices: 9.9 us -> 72.7 us
  blocking collectives: 51.2 us -> 0 us
  Pallas kernels: 0 us -> 31.3 us
  matrix products: 28 us -> 0 us
    all_gather x4 -> x1, waiting for transfers between devices: 197 us -> 0.02 us  [per_device(): down = lax.all_gather(down_weight.T, 'dp', axis=0, tiled=True)]
    all_to_all x1 -> x5, waiting for transfers between devices: 7.42 us -> 63.3 us  [the longest x1 38 us: per_device(): parts = lax.all_to_all(parts, 'head', 0, 0, tiled=True)]
    psum x3 -> x0, blocking collectives: 51.2 us -> none  [the longest x1 18.9 us: per_device(): final_dot = lax.psum(jnp.sum(norm_grad * resid, axis=1), 'head')]
    ppermute x0 -> x20, waiting for transfers between devices: none -> 39.6 us  [the longest x19 25 us: move(): return lax.ppermute(value, AXES, pairs)]
    reduce_scatter x1 -> x0, waiting for transfers between devices: 35 us -> none  [per_device(): lax.psum_scatter(term.astype(jnp.bfloat16), 'head', scatter_dimension=1,...]
    ppermute x0 -> x20, starting transfers between devices: none -> 33.8 us  [the longest x19 31.8 us: move(): return lax.ppermute(value, AXES, pairs)]
    pallas_call x0 -> x5, Pallas kernels: none -> 31.3 us  [the longest x1 10.8 us: per_device(): call(final_kernel, (jax.ShapeDtypeStruct((512, 896), BF), jax.ShapeDtypeS...]
    all_to_all x1 -> x5, starting transfers between devices: 9.7 us -> 38.9 us  [the longest x3 17.4 us: swap_rows(): lax.all_to_all(jnp.broadcast_to(value[None], (8,) + value.shape), 'head',...]
  transfers between devices with their start and end apart: 6 -> 26, of which waited for: 6 -> 8; matrix products, arithmetic and copies ran while one was open for 8% -> 8% of each run, Pallas kernels for 0% -> 5%
where the time goes in v1:
time: 247 us; the launch traced here: 245 us
  waiting for transfers between devices  104 us (42%)
  starting transfers between devices  72.7 us (29%)
  Pallas kernels  31.3 us (13%)
  between operations  14.4 us (6%)
  local copies, waits for them, and re-layouts  12.3 us (5%)
  other arithmetic  11.1 us (4%)
    all_to_all x1, waiting for transfers between devices, per_device(): parts = lax.all_to_all(parts, 'head', 0, 0, tiled=True)  38 us
    ppermute x19, starting transfers between devices, move(): return lax.ppermute(value, AXES, pairs)  31.8 us
    ppermute x19, waiting for transfers between devices, move(): return lax.ppermute(value, AXES, pairs)  25 us
    all_to_all x1, waiting for transfers between devices, per_device(): arrived = lax.all_to_all(outgoing, 'dp', 0, 0, tiled=True)  21.2 us
    all_to_all x3, starting transfers between devices, swap_rows(): lax.all_to_all(jnp.broadcast_to(value[None], (8,) + value.shape), 'head',...  17.4 us
    all_to_all x1, starting transfers between devices, per_device(): arrived = lax.all_to_all(outgoing, 'dp', 0, 0, tiled=True)  14.9 us
    ppermute x1, waiting for transfers between devices, spread_columns(): return lax.ppermute(shard, AXES, pairs)  14.6 us
    pallas_call x1, Pallas kernels, per_device(): call(final_kernel, (jax.ShapeDtypeStruct((512, 896), BF), jax.ShapeDtypeS...  10.8 us
  transfers between devices with their start and end apart: 26, of which 8 were waited for; matrix products, arithmetic and copies ran while one was open for 8% of the time, Pallas kernels for 5%

profile of v1, /device:TPU:33, one launch (start us, length us, event | category | flops | bytes accessed | tf_op | source)
XLA Modules:
  0.0 245.4 jit_solution(11786295535289336958)
XLA Ops:
  7.2 0.7 all-gather.2.cloned.1.call-update
  7.9 1.3 slice_bitcast_fusion.1
  9.4 1.3 collective-permute-start.9
  10.7 1.5 collective-permute-start.10
  12.2 1.9 collective-permute-start
  14.1 14.6 %collective-permute-done.w0 = bf16[112,1024]{1,0:T(8,128)(2,1)S(1)} collective-permute-done((bf16[112,1024]{1,0:T(8,128)(2,1)S(1)}, bf16[112,1024]{1,0:T(8,128)(2,1)S(1)}, u32[]{:S(2)}, u32[]{:S(2)}) %collective-permute-start) | collective-permute-done | bytes 229408 | tf_op jit(solution)/shard_map/ppermute | solution.py:39
  28.7 1.5 collective-permute-start.4
  30.2 5.5 %collective-permute-done.1.f1 = bf16[112,1024]{1,0:T(8,128)(2,1)S(1)} collective-permute-done((bf16[112,1024]{1,0:T(8,128)(2,1)S(1)}, bf16[112,1024]{1,0:T(8,128)(2,1)S(1)}, u32[]{:S(2)}, u32[]{:S(2)}) %collective-permute-start.1) | collective-permute-done | bytes 229408 | tf_op jit(solution)/shard_map/ppermute | solution.py:29
  35.6 1.5 collective-permute-start.5
  37.1 4.2 %collective-permute-start.11 = (bf16[256,1024]{1,0:T(8,128)(2,1)S(1)}, bf16[256,1024]{1,0:T(8,128)(2,1)S(1)}, u32[]{:S(2)}, u32[]{:S(2)}) collective-permute-start(bf16[256,1024]{1,0:T(8,128)(2,1)S(1)} %slice.62), channel_id=1, source_target_pairs={{0,64},{1,65},{2,66},{3,67},{4,68},{5,69},{6,70},{7,71},{8,72},{9,... | collective-permute-start | bytes 1572872 | tf_op jit(solution)/shard_map/ppermute | solution.py:29
  41.4 6.1 %collective-permute-done.10.r2 = bf16[512,1024]{1,0:T(8,128)(2,1)S(1)} collective-permute-done((bf16[512,1024]{1,0:T(8,128)(2,1)S(1)}, bf16[512,1024]{1,0:T(8,128)(2,1)S(1)}, u32[]{:S(2)}, u32[]{:S(2)}) %collective-permute-start.10) | collective-permute-done | bytes 1048608 | tf_op jit(solution)/shard_map/ppermute | solution.py:29
  47.6 0.9 copy-done.10
  48.5 2.7 %collective-permute-start.3 = (bf16[112,1024]{1,0:T(8,128)(2,1)}, bf16[112,1024]{1,0:T(8,128)(2,1)S(1)}, u32[]{:S(2)}, u32[]{:S(2)}) collective-permute-start(bf16[112,1024]{1,0:T(8,128)(2,1)} %collective-permute-done.2.f2), channel_id=1, source_target_pairs={{0,8},{1,9},{2,10},{3,11},{4,12},{5,13},{6,14},{7,15},{8,16},{9,17... | collective-permute-start | bytes 688136 | tf_op jit(solution)/shard_map/ppermute | solution.py:29
  51.4 0.6 broadcast_in_dim.43
  52.0 6.8 %all-to-all-start.2 = ((f32[8,1,512]{2,1,0:T(1,128)}), f32[8,1,512]{2,1,0:T(1,128)S(1)}, u32[]{:S(2)}, u32[]{:S(2)}) async-start(f32[8,1,512]{2,1,0:T(1,128)} %broadcast_in_dim.43), calls=%async_computation.2 | async-start | bytes 32768 | tf_op jit(solution)/shard_map/all_to_all | solution.py:147
  58.8 3.5 %collective-permute-start.7 = (bf16[64,1024]{1,0:T(8,128)(2,1)S(1)}, bf16[64,1024]{1,0:T(8,128)(2,1)S(1)}, u32[]{:S(2)}, u32[]{:S(2)}) collective-permute-start(bf16[64,1024]{1,0:T(8,128)(2,1)S(1)} %slice.60), channel_id=1, source_target_pairs={{0,8},{1,9},{2,10},{3,11},{4,12},{5,13},{6,14},{7,15},{8,16},{9,17... | collective-permute-start | bytes 393224 | tf_op jit(solution)/shard_map/ppermute | solution.py:29
  62.6 1.2 fusion.25.slot
  63.8 4.8 %collective-permute-done.8.ob = bf16[48,1024]{1,0:T(8,128)(2,1)S(1)} collective-permute-done((bf16[48,1024]{1,0:T(8,128)(2,1)S(1)}, bf16[48,1024]{1,0:T(8,128)(2,1)S(1)}, u32[]{:S(2)}, u32[]{:S(2)}) %collective-permute-start.8) | collective-permute-done | bytes 98336 | tf_op jit(solution)/shard_map/ppermute | solution.py:29
  69.4 8.8 %part.1 = bf16[8,112,2048]{2,1,0:T(8,128)(2,1)} custom-call(s32[8]{0:T(128)} %fusion.25.slot, bf16[112,1024]{1,0:T(8,128)(2,1)} %copy-done.22, bf16[112,1024]{1,0:T(8,128)(2,1)} %copy-done.23, bf16[112,1024]{1,0:T(8,128)(2,1)} %collective-permute-done.2.f2, bf16[112,1024]{1,0:T(8,128)(2,1)} %copy-done.14, bf16[112,1024]{1,0:T(8,128)(2,1)} %copy-done.24, ...), custom_call_target="tpu_custom_call" | custom-call | flops 3758096384 | bytes 6000000 | tf_op jit(solution)/shard_map/part/pallas_call | solution.py:226
  78.3 6.6 %all-to-all-start = ((bf16[8,112,2048]{2,1,0:T(8,128)(2,1)}), bf16[8,112,2048]{2,1,0:T(8,128)(2,1)}, u32[]{:S(2)}, u32[]{:S(2)}) async-start(bf16[8,112,2048]{2,1,0:T(8,128)(2,1)} %part.1), calls=%async_computation | async-start | bytes 7340032 | tf_op jit(solution)/shard_map/all_to_all | solution.py:235
  86.1 0.8 convert_reduce_fusion
  88.6 1.6 multiply_reduce_fusion.1
  90.1 38.0 %all-to-all-done.parts = bf16[8,112,2048]{2,1,0:T(8,128)(2,1)} async-done(((bf16[8,112,2048]{2,1,0:T(8,128)(2,1)}), bf16[8,112,2048]{2,1,0:T(8,128)(2,1)}, u32[]{:S(2)}, u32[]{:S(2)}) %all-to-all-start) | async-done | bytes 3670048 | tf_op jit(solution)/shard_map/all_to_all | solution.py:235
  128.2 0.6 broadcast_in_dim.75
  128.8 4.1 %all-to-all-start.3 = ((f32[8,2,512]{2,1,0:T(2,128)}), f32[8,2,512]{2,1,0:T(2,128)S(1)}, u32[]{:S(2)}, u32[]{:S(2)}) async-start(f32[8,2,512]{2,1,0:T(2,128)} %broadcast_in_dim.75), calls=%async_computation.3 | async-start | bytes 65536 | tf_op jit(solution)/shard_map/all_to_all | solution.py:147
  132.9 5.1 %send.1 = bf16[32,112,128]{2,1,0:T(8,128)(2,1)} custom-call(s32[4]{0:T(128)} %copy-done.16, bf16[8,112,2048]{2,1,0:T(8,128)(2,1)} %all-to-all-done.parts, s32[4,512]{1,0:T(4,128)} %broadcast_add_fusion.lane_pos), custom_call_target="tpu_custom_call" | custom-call | flops 469762048 | bytes 6000000 | tf_op jit(solution)/shard_map/send/pallas_call | solution.py:236
  138.0 14.9 %all-to-all-start.1 = ((bf16[32,112,128]{2,1,0:T(8,128)(2,1)}), bf16[32,112,128]{2,1,0:T(8,128)(2,1)S(1)}, u32[]{:S(2)}, u32[]{:S(2)}) async-start(bf16[32,112,128]{2,1,0:T(8,128)(2,1)} %send.1), calls=%async_computation.1 | async-start | bytes 1835008 | tf_op jit(solution)/shard_map/all_to_all | solution.py:245
  153.5 0.6 add.290.row_pos
  154.1 0.8 copy.25.gain_final
  154.9 0.9 copy.27.gain_post
  155.8 1.1 convert_bitcast_fusion.out_value
  156.9 21.2 %all-to-all-done.1.arrived = bf16[32,112,128]{2,1,0:T(8,128)(2,1)S(1)} async-done(((bf16[32,112,128]{2,1,0:T(8,128)(2,1)}), bf16[32,112,128]{2,1,0:T(8,128)(2,1)S(1)}, u32[]{:S(2)}, u32[]{:S(2)}) %all-to-all-start.1) | async-done | bytes 917536 | tf_op jit(solution)/shard_map/all_to_all | solution.py:245
  178.0 0.9 copy-done.1
  179.0 3.6 %recv.1 = (f32[448,512]{1,0:T(8,128)}, f32[2,512]{1,0:T(2,128)}) custom-call(bf16[32,112,128]{2,1,0:T(8,128)(2,1)} %copy-done.1, s32[1,512]{1,0:T(1,128)} %add.290.row_pos, f32[448,512]{1,0:T(8,128)} %get-tuple-element.29.resid, f32[448,512]{1,0:T(8,128)} %get-tuple-element.36.gout, f32[448,1]{1,0:T(8,128)} %copy.25.gain_final), custom_call_target="tpu_custom_call" | custom-call | flops 469762048 | bytes 6000000 | tf_op jit(solution)/shard_map/recv/pallas_call | solution.py:246
  182.6 1.4 broadcast_in_dim.76
  184.0 6.5 %all-to-all-start.4 = ((f32[8,2,512]{2,1,0:T(2,128)}), f32[8,2,512]{2,1,0:T(2,128)S(1)}, u32[]{:S(2)}, u32[]{:S(2)}) async-start(f32[8,2,512]{2,1,0:T(2,128)} %broadcast_in_dim.76), calls=%async_computation.4 | async-start | bytes 65536 | tf_op jit(solution)/shard_map/all_to_all | solution.py:147
  190.5 0.6 pad_maximum_fusion.2.stats
  191.1 4.1 %all-to-all-done.4.dots = f32[8,2,512]{2,1,0:T(2,128)S(1)} async-done(((f32[8,2,512]{2,1,0:T(2,128)}), f32[8,2,512]{2,1,0:T(2,128)S(1)}, u32[]{:S(2)}, u32[]{:S(2)}) %all-to-all-start.4) | async-done | bytes 32800 | tf_op jit(solution)/shard_map/all_to_all | solution.py:147
  195.2 0.6 copy-done.11
  195.8 3.0 %norm.1 = (bf16[512,448]{1,0:T(8,128)(2,1)}, bf16[448,512]{1,0:T(8,128)(2,1)}) custom-call(f32[448,512]{1,0:T(8,128)} %get-tuple-element.9.norm_grad, f32[448,512]{1,0:T(8,128)} %get-tuple-element.29.resid, f32[448,512]{1,0:T(8,128)} %convert_bitcast_fusion.out_value, f32[448,1]{1,0:T(8,128)} %copy.27.gain_post, f32[3,512]{1,0:T(4,128)} %pad_maximum_fusion.2.stats, ...), custom_call_target="tpu_custom_call" | custom-call | flops 4587520 | bytes 6000000 | tf_op jit(solution)/shard_map/norm/pallas_call | solution.py:255
  199.1 2.4 collective-permute-start.16
  201.6 0.6 fusion.21.heads
  202.2 1.3 collective-permute-start.13
  203.5 8.7 %collective-permute-done.14.p2 = bf16[448,512]{1,0:T(8,128)(2,1)S(1)} collective-permute-done((bf16[448,512]{1,0:T(8,128)(2,1)}, bf16[448,512]{1,0:T(8,128)(2,1)S(1)}, u32[]{:S(2)}, u32[]{:S(2)}) %collective-permute-start.14) | collective-permute-done | bytes 458784 | tf_op jit(solution)/shard_map/ppermute | solution.py:29
  212.2 10.9 %collective-permute-start.15 = (bf16[448,512]{1,0:T(8,128)(2,1)S(1)}, bf16[448,512]{1,0:T(8,128)(2,1)}, u32[]{:S(2)}, u32[]{:S(2)}) collective-permute-start(bf16[448,512]{1,0:T(8,128)(2,1)S(1)} %collective-permute-done.14.p2), channel_id=1, source_target_pairs={{0,1},{1,0},{2,3},{3,2},{4,5},{5,4},{6,7},{7,6},{8,9},{9,8},{10,11... | collective-permute-start | bytes 1376264 | tf_op jit(solution)/shard_map/ppermute | solution.py:29
  223.6 3.2 %convert_multiply_fusion = (f32[512,896]{1,0:T(8,128)}, f32[512,896]{1,0:T(8,128)}) fusion(bf16[512,896]{1,0:T(8,128)(2,1)S(1)} %copy-done.3, bf16[512,896]{1,0:T(8,128)(2,1)S(1)} %copy-done.4), kind=kLoop, calls=%fused_computation.4 | loop fusion | flops 9633792 | bytes 5505024 | tf_op jit(solution)/shard_map/jvp()/mul | solution.py:141
  226.8 1.0 copy.28
  227.8 10.8 %final.1 = (bf16[512,896]{1,0:T(8,128)(2,1)}, bf16[512,896]{1,0:T(8,128)(2,1)}) custom-call(s32[8]{0:T(128)} %fusion.21.heads, bf16[448,512]{1,0:T(8,128)(2,1)} %get-tuple-element.12.p0, bf16[448,512]{1,0:T(8,128)(2,1)} %collective-permute-done.13.p1, bf16[448,512]{1,0:T(8,128)(2,1)} %copy-done.7, bf16[448,512]{1,0:T(8,128)(2,1)} %collective-permute-done.15.p3, ...), custom_call_target="tpu_custom_call" | custom-call | flops 3288334336 | bytes 6000000 | tf_op jit(solution)/shard_map/final/pallas_call | solution.py:269
  (115 shorter events, 6.1 us)
Async XLA Ops:
  7.2 220.6 %all-gather.2.cloned.1.call-start = ((), (), s32[]{:S(2)}) async-start(), calls=%async_computation.5 | async-start | bytes 6623232 | tf_op jit(solution)/shard_map/all_gather | solution.py:222
  7.9 4.2 %copy-start.12 = (bf16[2,112,256]{2,1,0:T(8,128)(2,1)S(1)}, bf16[2,112,256]{2,1,0:T(8,128)(2,1)}, u32[]{:S(2)}) copy-start(bf16[2,112,256]{2,1,0:T(8,128)(2,1)} %param.17) | copy-start | bytes 344068
  7.9 4.2 %copy-start.13 = (bf16[2,112,256]{2,1,0:T(8,128)(2,1)S(1)}, bf16[2,112,256]{2,1,0:T(8,128)(2,1)}, u32[]{:S(2)}) copy-start(bf16[2,112,256]{2,1,0:T(8,128)(2,1)} %param.16) | copy-start | bytes 344068
  9.4 49.5 %copy-start.2 = (bf16[512,1024]{1,0:T(8,128)(2,1)}, bf16[512,1024]{1,0:T(8,128)(2,1)S(1)}, u32[]{:S(2)}) copy-start(bf16[512,1024]{1,0:T(8,128)(2,1)S(1)} %pad_maximum_fusion.r0) | copy-start | bytes 3145732
  9.4 41.9 %copy-start = (bf16[512,448]{0,1:T(8,128)(2,1)S(1)}, bf16[512,448]{0,1:T(8,128)(2,1)}, u32[]{:S(2)}) copy-start(bf16[512,448]{0,1:T(8,128)(2,1)} %param.20) | copy-start | bytes 1376260
  9.4 27.7 %collective-permute-start.9 = (bf16[512,1024]{1,0:T(8,128)(2,1)S(1)}, bf16[512,1024]{1,0:T(8,128)(2,1)S(1)}, u32[]{:S(2)}, u32[]{:S(2)}) collective-permute-start(bf16[512,1024]{1,0:T(8,128)(2,1)S(1)} %pad_maximum_fusion.r0), channel_id=1, source_target_pairs={{0,64},{1,65},{2,66},{3,67},{4,68},{5,69},{6,70},{7,71},{8,72},{9,... | collective-permute-start | bytes 3145736 | tf_op jit(solution)/shard_map/ppermute | solution.py:29
  10.7 36.8 %collective-permute-start.10 = (bf16[512,1024]{1,0:T(8,128)(2,1)S(1)}, bf16[512,1024]{1,0:T(8,128)(2,1)S(1)}, u32[]{:S(2)}, u32[]{:S(2)}) collective-permute-start(bf16[512,1024]{1,0:T(8,128)(2,1)S(1)} %pad_maximum_fusion.r0), channel_id=1, source_target_pairs={{0,192},{1,193},{2,194},{3,195},{4,196},{5,197},{6,198},{7,199},{8... | collective-permute-start | bytes 3145736 | tf_op jit(solution)/shard_map/ppermute | solution.py:29
  12.2 16.5 %collective-permute-start = (bf16[112,1024]{1,0:T(8,128)(2,1)S(1)}, bf16[112,1024]{1,0:T(8,128)(2,1)S(1)}, u32[]{:S(2)}, u32[]{:S(2)}) collective-permute-start(bf16[112,1024]{1,0:T(8,128)(2,1)S(1)} %pad_maximum_fusion.1), channel_id=1, source_target_pairs={{0,0},{1,1},{2,2},{3,3},{4,4},{5,5},{6,6},{7,7},{8,64},{9,65},{10,... | collective-permute-start | bytes 688136 | tf_op jit(solution)/shard_map/ppermute | solution.py:39
  28.7 22.5 %copy-start.22 = (bf16[112,1024]{1,0:T(8,128)(2,1)}, bf16[112,1024]{1,0:T(8,128)(2,1)S(1)}, u32[]{:S(2)}) copy-start(bf16[112,1024]{1,0:T(8,128)(2,1)S(1)} %collective-permute-done.w0) | copy-start | bytes 688132
  28.7 6.9 %collective-permute-start.1 = (bf16[112,1024]{1,0:T(8,128)(2,1)S(1)}, bf16[112,1024]{1,0:T(8,128)(2,1)S(1)}, u32[]{:S(2)}, u32[]{:S(2)}) collective-permute-start(bf16[112,1024]{1,0:T(8,128)(2,1)S(1)} %collective-permute-done.w0), channel_id=1, source_target_pairs={{0,8},{1,9},{2,10},{3,11},{4,12},{5,13},{6,14},{7,15},{8,16},{9,17... | collective-permute-start | bytes 688136 | tf_op jit(solution)/shard_map/ppermute | solution.py:29
  28.7 6.9 %collective-permute-start.4 = (bf16[112,1024]{1,0:T(8,128)(2,1)S(1)}, bf16[112,1024]{1,0:T(8,128)(2,1)S(1)}, u32[]{:S(2)}, u32[]{:S(2)}) collective-permute-start(bf16[112,1024]{1,0:T(8,128)(2,1)S(1)} %collective-permute-done.w0), channel_id=1, source_target_pairs={{0,56},{1,57},{2,58},{3,59},{4,60},{5,61},{6,62},{7,63},{8,0},{9,1... | collective-permute-start | bytes 688136 | tf_op jit(solution)/shard_map/ppermute | solution.py:29
  35.6 12.0 %copy-start.23 = (bf16[112,1024]{1,0:T(8,128)(2,1)}, bf16[112,1024]{1,0:T(8,128)(2,1)S(1)}, u32[]{:S(2)}) copy-start(bf16[112,1024]{1,0:T(8,128)(2,1)S(1)} %collective-permute-done.1.f1) | copy-start | bytes 688132
  35.6 12.0 %collective-permute-start.2 = (bf16[112,1024]{1,0:T(8,128)(2,1)S(1)}, bf16[112,1024]{1,0:T(8,128)(2,1)}, u32[]{:S(2)}, u32[]{:S(2)}) collective-permute-start(bf16[112,1024]{1,0:T(8,128)(2,1)S(1)} %collective-permute-done.1.f1), channel_id=1, source_target_pairs={{0,8},{1,9},{2,10},{3,11},{4,12},{5,13},{6,14},{7,15},{8,16},{9,17... | collective-permute-start | bytes 688136 | tf_op jit(solution)/shard_map/ppermute | solution.py:29
  35.6 15.5 %copy-start.24 = (bf16[112,1024]{1,0:T(8,128)(2,1)}, bf16[112,1024]{1,0:T(8,128)(2,1)S(1)}, u32[]{:S(2)}) copy-start(bf16[112,1024]{1,0:T(8,128)(2,1)S(1)} %collective-permute-done.4.g1) | copy-start | bytes 688132
  35.6 15.5 %collective-permute-start.5 = (bf16[112,1024]{1,0:T(8,128)(2,1)S(1)}, bf16[112,1024]{1,0:T(8,128)(2,1)}, u32[]{:S(2)}, u32[]{:S(2)}) collective-permute-start(bf16[112,1024]{1,0:T(8,128)(2,1)S(1)} %collective-permute-done.4.g1), channel_id=1, source_target_pairs={{0,56},{1,57},{2,58},{3,59},{4,60},{5,61},{6,62},{7,63},{8,0},{9,1... | collective-permute-start | bytes 688136 | tf_op jit(solution)/shard_map/ppermute | solution.py:29
  37.1 10.5 %copy-start.9 = (bf16[512,1024]{1,0:T(8,128)(2,1)}, bf16[512,1024]{1,0:T(8,128)(2,1)S(1)}, u32[]{:S(2)}) copy-start(bf16[512,1024]{1,0:T(8,128)(2,1)S(1)} %collective-permute-done.9.r1) | copy-start | bytes 3145732
  37.1 31.5 %collective-permute-start.11 = (bf16[256,1024]{1,0:T(8,128)(2,1)S(1)}, bf16[256,1024]{1,0:T(8,128)(2,1)S(1)}, u32[]{:S(2)}, u32[]{:S(2)}) collective-permute-start(bf16[256,1024]{1,0:T(8,128)(2,1)S(1)} %slice.62), channel_id=1, source_target_pairs={{0,64},{1,65},{2,66},{3,67},{4,68},{5,69},{6,70},{7,71},{8,72},{9,... | collective-permute-start | bytes 1572872 | tf_op jit(solution)/shard_map/ppermute | solution.py:29
  47.4 1.0 copy-start.10
  47.5 21.1 %collective-permute-start.12 = (bf16[256,1024]{1,0:T(8,128)(2,1)S(1)}, bf16[256,1024]{1,0:T(8,128)(2,1)}, u32[]{:S(2)}, u32[]{:S(2)}) collective-permute-start(bf16[256,1024]{1,0:T(8,128)(2,1)S(1)} %slice.63), channel_id=1, source_target_pairs={{0,192},{1,193},{2,194},{3,195},{4,196},{5,197},{6,198},{7,199},{8... | collective-permute-start | bytes 1572872 | tf_op jit(solution)/shard_map/ppermute | solution.py:29
  48.5 10.3 %collective-permute-start.3 = (bf16[112,1024]{1,0:T(8,128)(2,1)}, bf16[112,1024]{1,0:T(8,128)(2,1)S(1)}, u32[]{:S(2)}, u32[]{:S(2)}) collective-permute-start(bf16[112,1024]{1,0:T(8,128)(2,1)} %collective-permute-done.2.f2), channel_id=1, source_target_pairs={{0,8},{1,9},{2,10},{3,11},{4,12},{5,13},{6,14},{7,15},{8,16},{9,17... | collective-permute-start | bytes 688136 | tf_op jit(solution)/shard_map/ppermute | solution.py:29
  51.1 11.2 %collective-permute-start.6 = (bf16[112,1024]{1,0:T(8,128)(2,1)}, bf16[112,1024]{1,0:T(8,128)(2,1)S(1)}, u32[]{:S(2)}, u32[]{:S(2)}) collective-permute-start(bf16[112,1024]{1,0:T(8,128)(2,1)} %collective-permute-done.5.g2), channel_id=1, source_target_pairs={{0,56},{1,57},{2,58},{3,59},{4,60},{5,61},{6,62},{7,63},{8,0},{9,1... | collective-permute-start | bytes 688136 | tf_op jit(solution)/shard_map/ppermute | solution.py:29
  52.0 26.3 %all-to-all-start.2 = ((f32[8,1,512]{2,1,0:T(1,128)}), f32[8,1,512]{2,1,0:T(1,128)S(1)}, u32[]{:S(2)}, u32[]{:S(2)}) async-start(f32[8,1,512]{2,1,0:T(1,128)} %broadcast_in_dim.43), calls=%async_computation.2 | async-start | bytes 32768 | tf_op jit(solution)/shard_map/all_to_all | solution.py:147
  58.8 9.8 %copy-start.14 = (bf16[112,1024]{1,0:T(8,128)(2,1)}, bf16[112,1024]{1,0:T(8,128)(2,1)S(1)}, u32[]{:S(2)}) copy-start(bf16[112,1024]{1,0:T(8,128)(2,1)S(1)} %collective-permute-done.3.f3) | copy-start | bytes 688132
  58.8 9.8 %collective-permute-start.7 = (bf16[64,1024]{1,0:T(8,128)(2,1)S(1)}, bf16[64,1024]{1,0:T(8,128)(2,1)S(1)}, u32[]{:S(2)}, u32[]{:S(2)}) collective-permute-start(bf16[64,1024]{1,0:T(8,128)(2,1)S(1)} %slice.60), channel_id=1, source_target_pairs={{0,8},{1,9},{2,10},{3,11},{4,12},{5,13},{6,14},{7,15},{8,16},{9,17... | collective-permute-start | bytes 393224 | tf_op jit(solution)/shard_map/ppermute | solution.py:29
  62.3 6.3 %copy-start.15 = (bf16[112,1024]{1,0:T(8,128)(2,1)}, bf16[112,1024]{1,0:T(8,128)(2,1)S(1)}, u32[]{:S(2)}) copy-start(bf16[112,1024]{1,0:T(8,128)(2,1)S(1)} %collective-permute-done.6.g3) | copy-start | bytes 688132
  62.3 6.2 %collective-permute-start.8 = (bf16[48,1024]{1,0:T(8,128)(2,1)S(1)}, bf16[48,1024]{1,0:T(8,128)(2,1)S(1)}, u32[]{:S(2)}, u32[]{:S(2)}) collective-permute-start(bf16[48,1024]{1,0:T(8,128)(2,1)S(1)} %slice.61), channel_id=1, source_target_pairs={{0,56},{1,57},{2,58},{3,59},{4,60},{5,61},{6,62},{7,63},{8,0},{9,1... | collective-permute-start | bytes 294920 | tf_op jit(solution)/shard_map/ppermute | solution.py:29
  78.3 6.6 %copy-start.20 = (s32[1024]{0:T(1024)S(1)}, s32[1024]{0:T(1024)}, u32[]{:S(2)}) copy-start(s32[1024]{0:T(1024)} %param.18) | copy-start | bytes 12292
  78.3 9.7 %copy-start.17 = (bf16[448]{0:T(512)(128)(2,1)S(1)}, bf16[448]{0:T(512)(128)(2,1)}, u32[]{:S(2)}) copy-start(bf16[448]{0:T(512)(128)(2,1)} %param.21) | copy-start | bytes 2692
  78.3 10.3 %copy-start.6 = (bf16[512,448]{0,1:T(8,128)(2,1)S(1)}, bf16[512,448]{0,1:T(8,128)(2,1)}, u32[]{:S(2)}) copy-start(bf16[512,448]{0,1:T(8,128)(2,1)} %param.19) | copy-start | bytes 1376260
  78.3 49.9 %all-to-all-start = ((bf16[8,112,2048]{2,1,0:T(8,128)(2,1)}), bf16[8,112,2048]{2,1,0:T(8,128)(2,1)}, u32[]{:S(2)}, u32[]{:S(2)}) async-start(bf16[8,112,2048]{2,1,0:T(8,128)(2,1)} %part.1), calls=%async_computation | async-start | bytes 7340032 | tf_op jit(solution)/shard_map/all_to_all | solution.py:235
  87.6 45.4 %copy-start.16 = (s32[4]{0:T(128)}, s32[4]{0:T(128)S(1)}, u32[]{:S(2)}) copy-start(s32[4]{0:T(128)S(1)} %pad_add_fusion.xs) | copy-start | bytes 52
  128.8 9.2 %all-to-all-start.3 = ((f32[8,2,512]{2,1,0:T(2,128)}), f32[8,2,512]{2,1,0:T(2,128)S(1)}, u32[]{:S(2)}, u32[]{:S(2)}) async-start(f32[8,2,512]{2,1,0:T(2,128)} %broadcast_in_dim.75), calls=%async_computation.3 | async-start | bytes 65536 | tf_op jit(solution)/shard_map/all_to_all | solution.py:147
  138.0 16.1 %copy-start.18 = (bf16[448]{0:T(512)(128)(2,1)S(1)}, bf16[448]{0:T(512)(128)(2,1)}, u32[]{:S(2)}) copy-start(bf16[448]{0:T(512)(128)(2,1)} %param.22) | copy-start | bytes 2692
  138.0 40.0 %all-to-all-start.1 = ((bf16[32,112,128]{2,1,0:T(8,128)(2,1)}), bf16[32,112,128]{2,1,0:T(8,128)(2,1)S(1)}, u32[]{:S(2)}, u32[]{:S(2)}) async-start(bf16[32,112,128]{2,1,0:T(8,128)(2,1)} %send.1), calls=%async_computation.1 | async-start | bytes 1835008 | tf_op jit(solution)/shard_map/all_to_all | solution.py:245
  182.6 19.1 %copy-start.19 = (s32[8]{0:T(128)S(1)}, s32[8]{0:T(128)}, u32[]{:S(2)}) copy-start(s32[8]{0:T(128)} %constant.213.clone) | copy-start | bytes 100
  182.6 41.0 %copy-start.3 = (bf16[512,896]{1,0:T(8,128)(2,1)S(1)}, bf16[512,896]{1,0:T(8,128)(2,1)}, u32[]{:S(2)}) copy-start(bf16[512,896]{1,0:T(8,128)(2,1)} %param.23) | copy-start | bytes 2752516
  182.6 41.0 %copy-start.4 = (bf16[512,896]{1,0:T(8,128)(2,1)S(1)}, bf16[512,896]{1,0:T(8,128)(2,1)}, u32[]{:S(2)}) copy-start(bf16[512,896]{1,0:T(8,128)(2,1)} %param.24) | copy-start | bytes 2752516
  184.0 11.2 %all-to-all-start.4 = ((f32[8,2,512]{2,1,0:T(2,128)}), f32[8,2,512]{2,1,0:T(2,128)S(1)}, u32[]{:S(2)}, u32[]{:S(2)}) async-start(f32[8,2,512]{2,1,0:T(2,128)} %broadcast_in_dim.76), calls=%async_computation.4 | async-start | bytes 65536 | tf_op jit(solution)/shard_map/all_to_all | solution.py:147
  198.9 13.3 %collective-permute-start.14 = (bf16[448,512]{1,0:T(8,128)(2,1)}, bf16[448,512]{1,0:T(8,128)(2,1)S(1)}, u32[]{:S(2)}, u32[]{:S(2)}) collective-permute-start(bf16[448,512]{1,0:T(8,128)(2,1)} %get-tuple-element.12.p0), channel_id=1, source_target_pairs={{0,2},{1,3},{2,4},{3,5},{4,6},{5,7},{6,0},{7,1},{8,10},{9,11},{10,... | collective-permute-start | bytes 1376264 | tf_op jit(solution)/shard_map/ppermute | solution.py:29
  199.1 23.9 %collective-permute-start.16 = (bf16[448,512]{1,0:T(8,128)(2,1)}, bf16[448,512]{1,0:T(8,128)(2,1)S(1)}, u32[]{:S(2)}, u32[]{:S(2)}) collective-permute-start(bf16[448,512]{1,0:T(8,128)(2,1)} %get-tuple-element.12.p0), channel_id=1, source_target_pairs={{0,6},{1,7},{2,0},{3,1},{4,2},{5,3},{6,4},{7,5},{8,14},{9,15},{10,... | collective-permute-start | bytes 1376264 | tf_op jit(solution)/shard_map/ppermute | solution.py:29
  201.5 21.6 %collective-permute-start.18 = (bf16[448,512]{1,0:T(8,128)(2,1)}, bf16[448,512]{1,0:T(8,128)(2,1)}, u32[]{:S(2)}, u32[]{:S(2)}) collective-permute-start(bf16[448,512]{1,0:T(8,128)(2,1)} %get-tuple-element.12.p0), channel_id=1, source_target_pairs={{0,4},{1,5},{2,6},{3,7},{4,0},{5,1},{6,2},{7,3},{8,12},{9,13},{10,... | collective-permute-start | bytes 1376264 | tf_op jit(solution)/shard_map/ppermute | solution.py:29
  202.2 24.6 %copy-start.5 = (bf16[512,448]{1,0:T(8,128)(2,1)S(1)}, bf16[512,448]{1,0:T(8,128)(2,1)}, u32[]{:S(2)}) copy-start(bf16[512,448]{1,0:T(8,128)(2,1)} %get-tuple-element.24) | copy-start | bytes 1376260
  202.2 25.5 %collective-permute-start.13 = (bf16[448,512]{1,0:T(8,128)(2,1)}, bf16[448,512]{1,0:T(8,128)(2,1)}, u32[]{:S(2)}, u32[]{:S(2)}) collective-permute-start(bf16[448,512]{1,0:T(8,128)(2,1)} %get-tuple-element.12.p0), channel_id=1, source_target_pairs={{0,1},{1,0},{2,3},{3,2},{4,5},{5,4},{6,7},{7,6},{8,9},{9,8},{10,11... | collective-permute-start | bytes 1376264 | tf_op jit(solution)/shard_map/ppermute | solution.py:29
  212.2 14.6 %copy-start.7 = (bf16[448,512]{1,0:T(8,128)(2,1)}, bf16[448,512]{1,0:T(8,128)(2,1)S(1)}, u32[]{:S(2)}) copy-start(bf16[448,512]{1,0:T(8,128)(2,1)S(1)} %collective-permute-done.14.p2) | copy-start | bytes 1376260
  212.2 15.6 %collective-permute-start.15 = (bf16[448,512]{1,0:T(8,128)(2,1)S(1)}, bf16[448,512]{1,0:T(8,128)(2,1)}, u32[]{:S(2)}, u32[]{:S(2)}) collective-permute-start(bf16[448,512]{1,0:T(8,128)(2,1)S(1)} %collective-permute-done.14.p2), channel_id=1, source_target_pairs={{0,1},{1,0},{2,3},{3,2},{4,5},{5,4},{6,7},{7,6},{8,9},{9,8},{10,11... | collective-permute-start | bytes 1376264 | tf_op jit(solution)/shard_map/ppermute | solution.py:29
  223.1 3.7 %copy-start.8 = (bf16[448,512]{1,0:T(8,128)(2,1)}, bf16[448,512]{1,0:T(8,128)(2,1)S(1)}, u32[]{:S(2)}) copy-start(bf16[448,512]{1,0:T(8,128)(2,1)S(1)} %collective-permute-done.16.p4) | copy-start | bytes 1376260
  223.1 4.7 %collective-permute-start.17 = (bf16[448,512]{1,0:T(8,128)(2,1)S(1)}, bf16[448,512]{1,0:T(8,128)(2,1)}, u32[]{:S(2)}, u32[]{:S(2)}) collective-permute-start(bf16[448,512]{1,0:T(8,128)(2,1)S(1)} %collective-permute-done.16.p4), channel_id=1, source_target_pairs={{0,1},{1,0},{2,3},{3,2},{4,5},{5,4},{6,7},{7,6},{8,9},{9,8},{10,11... | collective-permute-start | bytes 1376264 | tf_op jit(solution)/shard_map/ppermute | solution.py:29
  223.2 4.6 %collective-permute-start.19 = (bf16[448,512]{1,0:T(8,128)(2,1)}, bf16[448,512]{1,0:T(8,128)(2,1)}, u32[]{:S(2)}, u32[]{:S(2)}) collective-permute-start(bf16[448,512]{1,0:T(8,128)(2,1)} %collective-permute-done.18.p6), channel_id=1, source_target_pairs={{0,1},{1,0},{2,3},{3,2},{4,5},{5,4},{6,7},{7,6},{8,9},{9,8},{10,11... | collective-permute-start | bytes 1376264 | tf_op jit(solution)/shard_map/ppermute | solution.py:29
  (5 other events, 3.7 us)
Sparse Core Ops, SparseCore 0:
  10.6 92.4 all-gather.1

commit v2 on v1

v2 whole, which is shorter than its diff:
```python
import jax
import jax.numpy as jnp
from jax import lax
from jax.experimental import pallas as pl
from jax.experimental.pallas import tpu as pltpu
from jax.sharding import PartitionSpec as P

EPS = 1e-06
NX, NZ, NY, NC = 4, 8, 4, 2
AXES = ("dp", "head")
BF = jnp.bfloat16
F32 = jnp.float32
MIB = 56
W_FIRST = 0
R3 = 1
TIE = 1


def move(value, dx=0, dz=0, dy=0, dc=0):
    pairs = []
    for x in range(NX):
        for z in range(NZ):
            for y in range(NY):
                for c in range(NC):
                    src = (x * NZ + z) * 8 + y * NC + c
                    dst = (
                        ((x + dx) % NX * NZ + (z + dz) % NZ) * 8
                        + (y + dy) % NY * NC
                        + (c + dc) % NC
                    )
                    pairs.append((src, dst))
    return lax.ppermute(value, AXES, pairs)


def spread_columns(shard):
    pairs = []
    for x in range(NX):
        for z in range(NZ):
            for y in range(NY):
                for c in range(NC):
                    d, t = z // 4, z % 4
                    src = (x * NZ + z) * 8 + y * NC + c
                    pairs.append((src, (t * NZ + 4 * c + x) * 8 + y * NC + d))
    return lax.ppermute(shard, AXES, pairs)


def call(kernel, out_shape, n_scalar, n_array, flops, scratch=(), name=None, space=pltpu.VMEM):
    return pl.pallas_call(
        kernel,
        out_shape=out_shape,
        in_specs=[pl.BlockSpec(memory_space=pltpu.SMEM)] * n_scalar
        + [pl.BlockSpec(memory_space=space)] * n_array,
        out_specs=jax.tree.map(lambda _: pl.BlockSpec(memory_space=pltpu.VMEM), out_shape),
        scratch_shapes=scratch,
        compiler_params=pltpu.CompilerParams(vmem_limit_bytes=MIB * 1024 * 1024),
        cost_estimate=pl.CostEstimate(flops=flops, bytes_accessed=6_000_000, transcendentals=0),
        name=name,
    )


def dot_nt(a, b):
    return lax.dot_general(a, b, (((1,), (1,)), ((), ())), preferred_element_type=F32)


def dot_tn(a, b):
    return lax.dot_general(a, b, (((0,), (0,)), ((), ())), preferred_element_type=F32)


def part_kernel(where, core, *refs):
    pieces, out, wall, rows, sems = refs[:8], refs[-4], refs[-3], refs[-2], refs[-1]
    count = (len(refs) - 12) // 2
    copies = []
    for k, ref in enumerate(pieces):
        at = pl.multiple_of(where[k] % 4 * 112, 16)
        spot = wall.at[where[k] // 4, pl.ds(at, 112)]
        copies.append(pltpu.make_async_copy(ref, spot, sems.at[k]))
    at = 0
    for k in range(count):
        size = refs[8 + k].shape[0]
        for side in range(2):
            spot = rows.at[side, pl.ds(at, size)]
            ref, sem = refs[8 + side * count + k], sems.at[8 + 2 * k + side]
            copies.append(pltpu.make_async_copy(ref, spot, sem))
        at += size
    for copy in copies:
        copy.start()
    for copy in copies[:8]:
        copy.wait()
    own, other = wall[core[0]], wall[1 - core[0]]
    at = 0
    for k in range(count):
        size = refs[8 + k].shape[0]
        copies[8 + 2 * k].wait()
        copies[9 + 2 * k].wait()
        prod = dot_nt(own, rows[0, at : at + size, :])
        prod = (prod + dot_nt(other, rows[1, at : at + size, :])).astype(BF)
        for y in range(4):
            out[y, :, at : at + size] = prod[y * 112 : (y + 1) * 112, :]
        at += size


def send_kernel(xs, first, last, lane_pos, out, moved):
    for r in range(4):
        parts, at = (first, r * 512) if r < 3 else (last, 0)
        total = parts[0, :, at : at + 512].astype(F32)
        for g in range(1, 4):
            total = total + parts[g, :, at : at + 512].astype(F32)
        ids = lax.broadcasted_iota(jnp.int32, (1024, 512), 0)
        pick = jnp.where(ids == lane_pos[r : r + 1, :], 1.0, 0.0).astype(BF)
        moved[xs[r]] = dot_nt(total.astype(BF), pick).astype(BF)
    group = lax.broadcasted_iota(jnp.int32, (112, 128), 1) // 32
    for q in range(8):
        tiles = [moved[x, :, q * 128 : (q + 1) * 128] for x in range(4)]
        for j in range(4):
            here = tiles[(0 - j) % 4]
            for g in range(1, 4):
                here = jnp.where(group == g, tiles[(g - j) % 4], here)
            out[4 * q + j] = here


def recv_kernel(arrived, row_pos, resid, gout, gain_final, pair, grad, dots):
    ids = lax.broadcasted_iota(jnp.int32, (1024, 512), 0)
    pick = jnp.where(ids == row_pos[...], 1.0, 0.0).astype(BF)
    first = jnp.zeros((1, 512), F32)
    second = jnp.zeros((1, 512), F32)
    for x in range(4):
        side = jnp.concatenate([arrived[x * 8 + z] for z in range(8)], axis=1)
        rows = pl.ds(x * 112, 112)
        piece = jnp.dot(side, pick, preferred_element_type=F32)
        piece = piece * gain_final[rows, :]
        grad[rows, :] = piece
        first = first + jnp.sum(piece * resid[rows, :], axis=0, keepdims=True)
        second = second + jnp.sum(piece * gout[rows, :], axis=0, keepdims=True)
    for k in range(8):
        dots[k, 0:1, :] = first
        dots[k, 1:2, :] = second
        dots[k, 2:4, :] = pair[...]


def norm_kernel(norm_grad, resid, out_value, gain_post, out_scale, dots, resid_grad, post_grad):
    width = 3584.0
    sums = dots[0]
    for k in range(1, 8):
        sums = sums + dots[k]
    out_scale = out_scale[...]
    resid_scale = lax.rsqrt(sums[2:3, :] / width + EPS)
    final_mean = resid_scale * sums[0:1, :] / width
    post_dot = resid_scale * (sums[1:2, :] - resid_scale * final_mean * sums[3:4, :])
    post_mean = out_scale * post_dot / width
    total = resid_scale * (norm_grad[...] - resid[...] * (resid_scale * final_mean))
    post = out_scale * (total * gain_post[...] - out_value[...] * (out_scale * post_mean))
    post_grad[...] = post.astype(BF)
    resid_grad[...] = total.T.astype(BF)


def final_kernel(heads, *refs):
    posts, (weight, slope, active, gate, up) = refs[:8], refs[8:13]
    post_buf, weight_buf, scale_buf, sems = refs[13:]
    copies = []
    for k in range(8):
        at = pl.multiple_of(heads[k] * 448, 64)
        copies.append(pltpu.make_async_copy(posts[k], post_buf.at[k], sems.at[2 * k]))
        rows = weight.at[pl.ds(at, 448)]
        copies.append(pltpu.make_async_copy(rows, weight_buf.at[k], sems.at[2 * k + 1]))
    copies.append(pltpu.make_async_copy(slope, scale_buf.at[0], sems.at[16]))
    copies.append(pltpu.make_async_copy(active, scale_buf.at[1], sems.at[17]))
    for copy in copies:
        copy.start()
    value = jnp.zeros((512, 896), F32)
    for k in range(8):
        copies[2 * k].wait()
        copies[2 * k + 1].wait()
        value = value + dot_tn(post_buf[k], weight_buf[k])
    copies[16].wait()
    copies[17].wait()
    gate[...] = (value * scale_buf[0]).astype(BF)
    up[...] = (value * scale_buf[1]).astype(BF)


def gelu_parts(gate_value):
    activated, pullback = jax.vjp(
        lambda pre_act: jax.nn.gelu(pre_act, approximate=True), gate_value
    )
    return (activated, pullback(jnp.ones_like(gate_value))[0])


def swap_rows(value):
    return lax.all_to_all(
        jnp.broadcast_to(value[None], (8,) + value.shape), "head", 0, 0, tiled=True
    )


def per_device(
    key_grads,
    value_grads,
    key_weight,
    value_weight,
    block_source,
    hidden_mid,
    mlp_out,
    post_gain,
    final_gain,
    gate_pre,
    up_pre,
    down_weight,
):
    dev = lax.axis_index("dp")
    head = lax.axis_index("head")
    x, z = dev // NZ, dev % NZ
    y, c = head // NC, head % NC

    weight = jnp.concatenate([key_weight[0], key_weight[1], value_weight[0], value_weight[1]], 1)
    rows = jnp.concatenate([key_grads[0], key_grads[1], value_grads[0], value_grads[1]], 1)
    block_ids = jnp.arange(1024, dtype=jnp.int32)
    is_source = block_source[:, None] == block_ids[None, :]
    dest_block = jnp.sum(jnp.where(is_source, block_ids[:, None], 0), axis=0)
    dest_device = (dest_block // 32).reshape(32, 32)
    same_dest = dest_device[:, :, None] == dest_device[:, None, :]
    slot_ids = jnp.arange(32, dtype=jnp.int32)
    before = slot_ids[None, :] < slot_ids[:, None]
    rank = jnp.sum((same_dest & before[None]).astype(jnp.int32), axis=2)
    own_x = jnp.stack([x, (x + 3) % 4, (x + 1) % 4, (x + 2) % 4]).astype(jnp.int32)
    spread_ids = (own_x * NZ + z)[:, None, None] == slot_ids[None, :, None]
    dest_own = jnp.sum(jnp.where(spread_ids, dest_device[None], 0), axis=1)
    rank_own = jnp.sum(jnp.where(spread_ids, rank[None], 0), axis=1)
    lanes = (
        (dest_own // 4) * 128 + ((dest_own % 4 + own_x[:, None]) % 4) * 32 + rank_own * 16
    )
    lane_pos = (lanes[:, :, None] + jnp.arange(16, dtype=jnp.int32)).reshape(4, 512)
    source = lax.dynamic_slice_in_dim(block_source, dev * 32, 32)
    source_dev = source // 32
    source_rank = jnp.sum(
        jnp.where(block_ids[None, :] == source[:, None], rank.reshape(-1)[None, :], 0), axis=1
    )
    spot = (
        (source_dev % NZ) * 128 + ((dev % 4 + source_dev // NZ) % 4) * 32 + source_rank * 16
    )
    row_pos = (spot[:, None] + jnp.arange(16, dtype=jnp.int32)).reshape(1, 512)

    where = ((z - jnp.array([0, 1, 2, 3, 4, -1, -2, -3], jnp.int32)) % NZ).astype(jnp.int32)
    core = c.reshape(1).astype(jnp.int32)

    w0 = spread_columns(weight)
    s0 = move(rows, dc=1)
    gain_post = post_gain.astype(F32)[:, None]
    gain_final = final_gain.astype(F32)[:, None]
    out_value = mlp_out.T.astype(F32)
    sum_out = swap_rows(jnp.sum(out_value * out_value, axis=0)[None])
    w0, sum_out, where = lax.optimization_barrier((w0, sum_out, where))
    if W_FIRST:
        w0, rows = lax.optimization_barrier((w0, rows))
    r1, r2 = move(rows, dx=1), move(rows, dx=-1)
    if R3 == 0:
        r3 = move(rows, dx=2)
    f1, g1 = move(w0, dz=1), move(w0, dz=-1)
    f2, g2 = move(f1, dz=1), move(g1, dz=-1)
    f3, g3 = move(f2, dz=1), move(g2, dz=-1)
    if TIE:
        r1, r2, f3, g3, s0 = lax.optimization_barrier((r1, r2, f3, g3, s0))
    f4 = move(f3, dz=1)
    s1, s2 = move(r1, dc=1), move(r2, dc=1)
    if R3 == 0:
        s3 = move(r3, dc=1)
        far_rows, far_swapped = (r3,), (s3,)
    else:
        r3a, r3b = move(r1[:256], dx=1), move(r2[256:], dx=-1)
        s3a, s3b = move(r3a, dc=1), move(r3b, dc=1)
        far_rows, far_swapped = (r3a, r3b), (s3a, s3b)

    mid_value = hidden_mid.T.astype(F32)
    out_scale = lax.rsqrt(jnp.sum(sum_out, axis=0) / 3584 + EPS)
    gout = out_value * gain_post
    resid = mid_value + gout * out_scale
    pair = jnp.stack([jnp.sum(resid * resid, axis=0), jnp.sum(resid * gout, axis=0)])
    active, slope = gelu_parts(gate_pre.astype(F32))
    slope = slope * up_pre.astype(F32)
    down_share, r1 = lax.optimization_barrier((down_weight.T, r1))
    down = lax.all_gather(down_share, "dp", axis=0, tiled=True)

    pieces = (w0, f1, f2, f3, f4, g1, g2, g3)

    def part(left, right):
        size = sum(ref.shape[0] for ref in left)
        parts = call(
            part_kernel,
            jax.ShapeDtypeStruct((4, 112, size), BF),
            2,
            8 + 2 * len(left),
            2 * size * 448 * 2048,
            [
                pltpu.VMEM((2, 448, 1024), BF),
                pltpu.VMEM((2, size, 1024), BF),
                pltpu.SemaphoreType.DMA((8 + 2 * len(left),)),
            ],
            name="part",
            space=pl.ANY,
        )(where, core, *pieces, *left, *right)
        return lax.all_to_all(
            parts, "head", 0, 0, axis_index_groups=[[0, 2, 4, 6], [1, 3, 5, 7]], tiled=True
        )

    first = part((rows, r1, r2), (s0, s1, s2))
    last = part(far_rows, far_swapped)
    first, lane_pos, row_pos = lax.optimization_barrier((first, lane_pos, row_pos))
    outgoing = call(
        send_kernel,
        jax.ShapeDtypeStruct((32, 112, 128), BF),
        1,
        3,
        2 * 112 * 2048 * 1024,
        [pltpu.VMEM((4, 112, 1024), BF)],
        name="send",
    )(own_x, first, last, lane_pos)
    arrived = lax.all_to_all(outgoing, "dp", 0, 0, tiled=True)
    arrived, resid, gout, pair, out_scale, active, slope = lax.optimization_barrier(
        (arrived, resid, gout, pair, out_scale, active, slope)
    )
    norm_grad, dots = call(
        recv_kernel,
        (jax.ShapeDtypeStruct((448, 512), F32), jax.ShapeDtypeStruct((8, 4, 512), F32)),
        0,
        6,
        2 * 448 * 512 * 1024,
        name="recv",
    )(arrived, row_pos, resid, gout, gain_final, pair)
    dots = lax.all_to_all(dots, "head", 0, 0, tiled=True)
    resid_grad, post = call(
        norm_kernel,
        (jax.ShapeDtypeStruct((512, 448), BF), jax.ShapeDtypeStruct((448, 512), BF)),
        0,
        6,
        448 * 512 * 20,
        name="norm",
    )(norm_grad, resid, out_value, gain_post, out_scale, dots)
    p1, p2, p3 = move(post, dy=1), move(post, dy=-1), move(post, dy=2)
    q0 = move(post, dc=1)
    q1, q2, q3 = move(p1, dc=1), move(p2, dc=1), move(p3, dc=1)
    from_y = jnp.stack([y, y, y + 3, y + 3, y + 1, y + 1, y + 2, y + 2]) % 4
    from_c = (c + jnp.array([0, 1] * 4, jnp.int32)) % 2
    heads = (from_y * 2 + from_c).astype(jnp.int32)
    gate_grad, up_grad = call(
        final_kernel,
        (jax.ShapeDtypeStruct((512, 896), BF), jax.ShapeDtypeStruct((512, 896), BF)),
        1,
        11,
        2 * 512 * 896 * 3584,
        [
            pltpu.VMEM((8, 448, 512), BF),
            pltpu.VMEM((8, 448, 896), BF),
            pltpu.VMEM((2, 512, 896), F32),
            pltpu.SemaphoreType.DMA((18,)),
        ],
        name="final",
        space=pl.ANY,
    )(heads, post, q0, p1, q1, p2, q2, p3, q3, down, slope, active)
    return (resid_grad, gate_grad, up_grad)


def solution(mesh):
    return jax.shard_map(
        per_device,
        mesh=mesh,
        in_specs=(
            P(None, "dp", "head"),
            P(None, "dp", "head"),
            P(None, "dp", "head"),
            P(None, "dp", "head"),
            P(),
            P("dp", "head"),
            P("dp", "head"),
            P("head"),
            P("head"),
            P("dp", "head"),
            P("dp", "head"),
            P("head", "dp"),
        ),
        out_specs=(P("dp", "head"), P("dp", "head"), P("dp", "head")),
        check_vma=False,
    )
```

time: 247 us -> 218 us (0.88)
  waiting for transfers between devices: 104 us -> 71 us
    all_to_all x1 -> x3, waiting for transfers between devices: 38 us -> 14.3 us  [the longest x2 11.3 us: part(): lax.all_to_all(parts, 'head', 0, 0, axis_index_groups=[[0, 2, 4, 6], [1,...]
    ppermute x1, waiting for transfers between devices: 14.6 us -> 0.01 us  [spread_columns(): return lax.ppermute(shard, AXES, pairs)]
    all_to_all x3 -> x1, starting transfers between devices: 17.4 us -> 4.58 us  [swap_rows(): lax.all_to_all(jnp.broadcast_to(value[None], (8,) + value.shape), 'head',...]
    all_to_all x1 -> x3, starting transfers between devices: 6.6 us -> 15.5 us  [the longest x1 7.82 us: per_device(): dots = lax.all_to_all(dots, 'head', 0, 0, tiled=True)]
    all_to_all x1, starting transfers between devices: 14.9 us -> 7.27 us  [per_device(): arrived = lax.all_to_all(outgoing, 'dp', 0, 0, tiled=True)]
    all_to_all x1, waiting for transfers between devices: 21.2 us -> 26.6 us  [per_device(): arrived = lax.all_to_all(outgoing, 'dp', 0, 0, tiled=True)]
    ppermute x19 -> x23, starting transfers between devices: 31.8 us -> 37.2 us  [move(): return lax.ppermute(value, AXES, pairs)]
    ppermute x1, starting transfers between devices: 1.92 us -> 7.08 us  [spread_columns(): return lax.ppermute(shard, AXES, pairs)]
  transfers between devices with their start and end apart: 26 -> 30, of which waited for: 8 -> 14; matrix products, arithmetic and copies ran while one was open for 8% -> 9% of each run, Pallas kernels for 5% -> 8%
where the time goes in v2:
time: 218 us; the launch traced here: 217 us
  starting transfers between devices  71.6 us (33%)
  waiting for transfers between devices  71 us (33%)
  Pallas kernels  33.6 us (15%)
  local copies, waits for them, and re-layouts  14.7 us (7%)
  between operations  14.4 us (7%)
  other arithmetic  11.5 us (5%)
    ppermute x23, starting transfers between devices, move(): return lax.ppermute(value, AXES, pairs)  37.2 us
    all_to_all x1, waiting for transfers between devices, per_device(): arrived = lax.all_to_all(outgoing, 'dp', 0, 0, tiled=True)  26.6 us
    ppermute x23, waiting for transfers between devices, move(): return lax.ppermute(value, AXES, pairs)  25.9 us
    pallas_call x2, Pallas kernels, part(): call(part_kernel, jax.ShapeDtypeStruct((4, 112, size), BF), 2, 8 + 2 * le...  13.5 us
    all_to_all x2, waiting for transfers between devices, part(): lax.all_to_all(parts, 'head', 0, 0, axis_index_groups=[[0, 2, 4, 6], [1,...  11.3 us
    pallas_call x1, Pallas kernels, per_device(): call(final_kernel, (jax.ShapeDtypeStruct((512, 896), BF), jax.ShapeDtypeS...  8.88 us
    all_to_all x1, starting transfers between devices, per_device(): dots = lax.all_to_all(dots, 'head', 0, 0, tiled=True)  7.82 us
    all_to_all x2, starting transfers between devices, part(): lax.all_to_all(parts, 'head', 0, 0, axis_index_groups=[[0, 2, 4, 6], [1,...  7.65 us
  transfers between devices with their start and end apart: 30, of which 14 were waited for; matrix products, arithmetic and copies ran while one was open for 9% of the time, Pallas kernels for 8%

profile of v2, /device:TPU:33, one launch (start us, length us, event | category | flops | bytes accessed | tf_op | source)
XLA Modules:
  0.0 216.9 jit_solution(8515561524284149614)
XLA Ops:
  7.2 1.3 slice_bitcast_fusion.1
  8.7 1.3 collective-permute-start.3
  10.0 1.5 collective-permute-start.4
  11.4 1.2 collective-permute-start.9
  12.7 7.1 %collective-permute-start = (bf16[112,1024]{1,0:T(8,128)(2,1)S(1)}, bf16[112,1024]{1,0:T(8,128)(2,1)S(1)}, u32[]{:S(2)}, u32[]{:S(2)}) collective-permute-start(bf16[112,1024]{1,0:T(8,128)(2,1)S(1)} %pad_maximum_fusion.1), channel_id=1, source_target_pairs={{0,0},{1,32},{2,2},{3,34},{4,4},{5,36},{6,6},{7,38},{8,64},{9,96},... | collective-permute-start | bytes 688136 | tf_op jit(solution)/shard_map/ppermute | solution.py:44
  20.6 4.6 %all-to-all-start = ((f32[8,1,512]{2,1,0:T(1,128)}), f32[8,1,512]{2,1,0:T(1,128)S(1)}, u32[]{:S(2)}, u32[]{:S(2)}) async-start(f32[8,1,512]{2,1,0:T(1,128)} %broadcast_in_dim.84), calls=%async_computation | async-start | bytes 32768 | tf_op jit(solution)/shard_map/all_to_all | solution.py:188
  25.7 4.2 %all-to-all-done = f32[8,1,512]{2,1,0:T(1,128)S(1)} async-done(((f32[8,1,512]{2,1,0:T(1,128)}), f32[8,1,512]{2,1,0:T(1,128)S(1)}, u32[]{:S(2)}, u32[]{:S(2)}) %all-to-all-start) | async-done | bytes 16416 | tf_op jit(solution)/shard_map/all_to_all | solution.py:188
  29.9 1.9 collective-permute-start.1
  31.7 4.7 %collective-permute-done.1.refs_1_ = bf16[112,1024]{1,0:T(8,128)(2,1)S(1)} collective-permute-done((bf16[112,1024]{1,0:T(8,128)(2,1)S(1)}, bf16[112,1024]{1,0:T(8,128)(2,1)S(1)}, u32[]{:S(2)}, u32[]{:S(2)}) %collective-permute-start.1) | collective-permute-done | bytes 229408 | tf_op jit(solution)/shard_map/ppermute | solution.py:32
  36.5 1.9 collective-permute-start.2
  38.4 1.6 collective-permute-done.6.refs_5_
  40.0 2.0 collective-permute-done.2.refs_2_
  41.9 3.5 %collective-permute-start.5 = (bf16[112,1024]{1,0:T(8,128)(2,1)S(1)}, bf16[112,1024]{1,0:T(8,128)(2,1)}, u32[]{:S(2)}, u32[]{:S(2)}) collective-permute-start(bf16[112,1024]{1,0:T(8,128)(2,1)S(1)} %collective-permute-done.2.refs_2_), channel_id=1, source_target_pairs={{0,8},{1,9},{2,10},{3,11},{4,12},{5,13},{6,14},{7,15},{8,16},{9,17... | collective-permute-start | bytes 688136 | tf_op jit(solution)/shard_map/ppermute | solution.py:32
  45.4 1.0 collective-permute-done.7.refs_6_
  46.4 2.8 %collective-permute-done.5.refs_3_ = bf16[112,1024]{1,0:T(8,128)(2,1)} collective-permute-done((bf16[112,1024]{1,0:T(8,128)(2,1)S(1)}, bf16[112,1024]{1,0:T(8,128)(2,1)}, u32[]{:S(2)}, u32[]{:S(2)}) %collective-permute-start.5) | collective-permute-done | bytes 229408 | tf_op jit(solution)/shard_map/ppermute | solution.py:32
  49.3 2.8 %collective-permute-done.8.refs_7_ = bf16[112,1024]{1,0:T(8,128)(2,1)S(1)} collective-permute-done((bf16[112,1024]{1,0:T(8,128)(2,1)S(1)}, bf16[112,1024]{1,0:T(8,128)(2,1)S(1)}, u32[]{:S(2)}, u32[]{:S(2)}) %collective-permute-start.8) | collective-permute-done | bytes 229408 | tf_op jit(solution)/shard_map/ppermute | solution.py:32
  52.8 2.5 %collective-permute-start.11 = (bf16[512,1024]{1,0:T(8,128)(2,1)}, bf16[512,1024]{1,0:T(8,128)(2,1)}, u32[]{:S(2)}, u32[]{:S(2)}) collective-permute-start(bf16[512,1024]{1,0:T(8,128)(2,1)} %collective-permute-done.3.refs_9_), channel_id=1, source_target_pairs={{0,1},{1,0},{2,3},{3,2},{4,5},{5,4},{6,7},{7,6},{8,9},{9,8},{10,11... | collective-permute-start | bytes 3145736 | tf_op jit(solution)/shard_map/ppermute | solution.py:32
  56.0 3.1 %collective-permute-start.10 = (bf16[112,1024]{1,0:T(8,128)(2,1)}, bf16[112,1024]{1,0:T(8,128)(2,1)S(1)}, u32[]{:S(2)}, u32[]{:S(2)}) collective-permute-start(bf16[112,1024]{1,0:T(8,128)(2,1)} %collective-permute-done.5.refs_3_), channel_id=1, source_target_pairs={{0,8},{1,9},{2,10},{3,11},{4,12},{5,13},{6,14},{7,15},{8,16},{9,17... | collective-permute-start | bytes 688136 | tf_op jit(solution)/shard_map/ppermute | solution.py:32
  59.9 1.1 slice.38
  61.0 1.9 slice.39
  62.8 2.7 %collective-permute-start.14 = (bf16[256,1024]{1,0:T(8,128)(2,1)}, bf16[256,1024]{1,0:T(8,128)(2,1)S(1)}, u32[]{:S(2)}, u32[]{:S(2)}) collective-permute-start(bf16[256,1024]{1,0:T(8,128)(2,1)} %slice.39), channel_id=1, source_target_pairs={{0,192},{1,193},{2,194},{3,195},{4,196},{5,197},{6,198},{7,199},{8... | collective-permute-start | bytes 1572872 | tf_op jit(solution)/shard_map/ppermute | solution.py:32
  66.2 7.8 %part.2 = bf16[4,112,1536]{2,1,0:T(8,128)(2,1)} custom-call(s32[8]{0:T(128)} %and_select_fusion.6.where, s32[1]{0:T(128)} %bitcast.9.core, bf16[112,1024]{1,0:T(8,128)(2,1)} %copy-done.18, bf16[112,1024]{1,0:T(8,128)(2,1)} %copy-done.19, bf16[112,1024]{1,0:T(8,128)(2,1)} %copy-done.21, bf16[112,1024]{1,0:T(8,128)(2,1)} %collective-permute-done.5.refs_3_, ...), custom_call_target="tpu_custom_call" | custom-call | flops 2818572288 | bytes 6000000 | tf_op jit(solution)/shard_map/part/pallas_call | solution.py:284
  74.0 4.2 %all-to-all-start.1 = ((bf16[4,112,1536]{2,1,0:T(8,128)(2,1)}), bf16[4,112,1536]{2,1,0:T(8,128)(2,1)S(1)}, u32[]{:S(2)}, u32[]{:S(2)}) async-start(bf16[4,112,1536]{2,1,0:T(8,128)(2,1)} %part.2), calls=%async_computation.1 | async-start | bytes 2752512 | tf_op jit(solution)/shard_map/all_to_all | solution.py:298
  78.6 2.1 collective-permute-start.15
  82.2 0.9 collective-permute-done.16.refs_11_
  83.1 5.7 %part.3 = bf16[4,112,512]{2,1,0:T(8,128)(2,1)} custom-call(s32[8]{0:T(128)} %and_select_fusion.6.where, s32[1]{0:T(128)} %bitcast.9.core, bf16[112,1024]{1,0:T(8,128)(2,1)} %copy-done.18, bf16[112,1024]{1,0:T(8,128)(2,1)} %copy-done.19, bf16[112,1024]{1,0:T(8,128)(2,1)} %copy-done.21, bf16[112,1024]{1,0:T(8,128)(2,1)} %collective-permute-done.5.refs_3_, ...), custom_call_target="tpu_custom_call" | custom-call | flops 939524096 | bytes 6000000 | tf_op jit(solution)/shard_map/part/pallas_call | solution.py:284
  88.8 6.1 %all-to-all-done.1.first = bf16[4,112,1536]{2,1,0:T(8,128)(2,1)S(1)} async-done(((bf16[4,112,1536]{2,1,0:T(8,128)(2,1)}), bf16[4,112,1536]{2,1,0:T(8,128)(2,1)S(1)}, u32[]{:S(2)}, u32[]{:S(2)}) %all-to-all-start.1) | async-done | bytes 1376288 | tf_op jit(solution)/shard_map/all_to_all | solution.py:298
  95.0 3.5 %all-to-all-start.2 = ((bf16[4,112,512]{2,1,0:T(8,128)(2,1)}), bf16[4,112,512]{2,1,0:T(8,128)(2,1)S(1)}, u32[]{:S(2)}, u32[]{:S(2)}) async-start(bf16[4,112,512]{2,1,0:T(8,128)(2,1)} %part.3), calls=%async_computation.2 | async-start | bytes 917504 | tf_op jit(solution)/shard_map/all_to_all | solution.py:298
  99.8 5.2 %all-to-all-done.2.last = bf16[4,112,512]{2,1,0:T(8,128)(2,1)S(1)} async-done(((bf16[4,112,512]{2,1,0:T(8,128)(2,1)}), bf16[4,112,512]{2,1,0:T(8,128)(2,1)S(1)}, u32[]{:S(2)}, u32[]{:S(2)}) %all-to-all-start.2) | async-done | bytes 458784 | tf_op jit(solution)/shard_map/all_to_all | solution.py:298
  105.8 4.6 %send.1 = bf16[32,112,128]{2,1,0:T(8,128)(2,1)} custom-call(s32[4]{0:T(128)} %copy-done.28, bf16[4,112,1536]{2,1,0:T(8,128)(2,1)} %copy-done, bf16[4,112,512]{2,1,0:T(8,128)(2,1)} %copy-done.3, s32[4,512]{1,0:T(4,128)} %broadcast_add_fusion.lane_pos), custom_call_target="tpu_custom_call" | custom-call | flops 469762048 | bytes 6000000 | tf_op jit(solution)/shard_map/send/pallas_call | solution.py:305
  110.4 7.3 %all-to-all-start.3 = ((bf16[32,112,128]{2,1,0:T(8,128)(2,1)}), bf16[32,112,128]{2,1,0:T(8,128)(2,1)S(1)}, u32[]{:S(2)}, u32[]{:S(2)}) async-start(bf16[32,112,128]{2,1,0:T(8,128)(2,1)} %send.1), calls=%async_computation.3 | async-start | bytes 1835008 | tf_op jit(solution)/shard_map/all_to_all | solution.py:314
  117.7 0.8 copy.21.gain_final
  118.5 3.2 %fusion.3 = (f32[512,896]{1,0:T(8,128)}, f32[512,896]{1,0:T(8,128)}) fusion(bf16[512,896]{1,0:T(8,128)(2,1)S(1)} %copy-done.5, bf16[512,896]{1,0:T(8,128)(2,1)S(1)} %copy-done.6), kind=kLoop, calls=%fused_computation.10 | loop fusion | flops 9633792 | bytes 5505024 | tf_op jit(solution)/shard_map/mul | solution.py:276
  121.8 2.6 %multiply_reduce_fusion.1 = (f32[512]{0:T(512)S(1)}, f32[512]{0:T(512)S(1)}, f32[448,512]{1,0:T(8,128)}, f32[448,512]{1,0:T(8,128)}) fusion(f32[512]{0:T(512)S(1)} %add_rsqrt_fusion, f32[448]{0:T(512)S(1)} %convert_element_type.29, bf16[512,448]{0,1:T(8,128)(2,1)S(1)} %copy-done.1, bf16[512,448]{0,1:T(8,128)(2,1)} %param.19), kind=kLoop, calls=%fused_computation.19 | loop fusion | flops 2063360 | bytes 2760448 | tf_op jit(solution)/shard_map/reduce_sum | solution.py:274
  125.0 26.6 %all-to-all-done.3.arrived = bf16[32,112,128]{2,1,0:T(8,128)(2,1)S(1)} async-done(((bf16[32,112,128]{2,1,0:T(8,128)(2,1)}), bf16[32,112,128]{2,1,0:T(8,128)(2,1)S(1)}, u32[]{:S(2)}, u32[]{:S(2)}) %all-to-all-start.3) | async-done | bytes 917536 | tf_op jit(solution)/shard_map/all_to_all | solution.py:314
  151.6 0.9 copy-done.2
  152.5 3.6 %recv.1 = (f32[448,512]{1,0:T(8,128)}, f32[8,4,512]{2,1,0:T(4,128)}) custom-call(bf16[32,112,128]{2,1,0:T(8,128)(2,1)} %copy-done.2, s32[1,512]{1,0:T(1,128)} %add.267.row_pos, f32[448,512]{1,0:T(8,128)} %get-tuple-element.42.resid, f32[448,512]{1,0:T(8,128)} %get-tuple-element.43.gout, f32[448,1]{1,0:T(8,128)} %copy.21.gain_final, ...), custom_call_target="tpu_custom_call" | custom-call | flops 469762048 | bytes 6000000 | tf_op jit(solution)/shard_map/recv/pallas_call | solution.py:318
  156.1 7.8 %all-to-all-start.4 = ((f32[8,4,512]{2,1,0:T(4,128)}), f32[8,4,512]{2,1,0:T(4,128)S(1)}, u32[]{:S(2)}, u32[]{:S(2)}) async-start(f32[8,4,512]{2,1,0:T(4,128)} %get-tuple-element.47), calls=%async_computation.4 | async-start | bytes 131072 | tf_op jit(solution)/shard_map/all_to_all | solution.py:326
  163.9 1.0 convert_bitcast_fusion.out_value
  165.0 0.8 copy.22.gain_post
  165.8 3.0 %all-to-all-done.4.dots = f32[8,4,512]{2,1,0:T(4,128)S(1)} async-done(((f32[8,4,512]{2,1,0:T(4,128)}), f32[8,4,512]{2,1,0:T(4,128)S(1)}, u32[]{:S(2)}, u32[]{:S(2)}) %all-to-all-start.4) | async-done | bytes 65568 | tf_op jit(solution)/shard_map/all_to_all | solution.py:326
  169.4 3.1 %norm.1 = (bf16[512,448]{1,0:T(8,128)(2,1)}, bf16[448,512]{1,0:T(8,128)(2,1)}) custom-call(f32[448,512]{1,0:T(8,128)} %get-tuple-element.45.norm_grad, f32[448,512]{1,0:T(8,128)} %get-tuple-element.42.resid, f32[448,512]{1,0:T(8,128)} %convert_bitcast_fusion.out_value, f32[448,1]{1,0:T(8,128)} %copy.22.gain_post, f32[1,512]{1,0:T(1,128)} %bitcast.53, ...), custom_call_target="tpu_custom_call" | custom-call | flops 4587520 | bytes 6000000 | tf_op jit(solution)/shard_map/norm/pallas_call | solution.py:327
  172.8 2.4 %collective-permute-start.20 = (bf16[448,512]{1,0:T(8,128)(2,1)}, bf16[448,512]{1,0:T(8,128)(2,1)S(1)}, u32[]{:S(2)}, u32[]{:S(2)}) collective-permute-start(bf16[448,512]{1,0:T(8,128)(2,1)} %get-tuple-element.49.refs_0_), channel_id=1, source_target_pairs={{0,6},{1,7},{2,0},{3,1},{4,2},{5,3},{6,4},{7,5},{8,14},{9,15},{10,... | collective-permute-start | bytes 1376264 | tf_op jit(solution)/shard_map/ppermute | solution.py:32
  175.2 1.3 collective-permute-start.17
  176.5 9.3 %collective-permute-done.18.refs_2_ = bf16[448,512]{1,0:T(8,128)(2,1)S(1)} collective-permute-done((bf16[448,512]{1,0:T(8,128)(2,1)}, bf16[448,512]{1,0:T(8,128)(2,1)S(1)}, u32[]{:S(2)}, u32[]{:S(2)}) %collective-permute-start.18) | collective-permute-done | bytes 458784 | tf_op jit(solution)/shard_map/ppermute | solution.py:32
  185.8 10.9 %collective-permute-start.19 = (bf16[448,512]{1,0:T(8,128)(2,1)S(1)}, bf16[448,512]{1,0:T(8,128)(2,1)S(1)}, u32[]{:S(2)}, u32[]{:S(2)}) collective-permute-start(bf16[448,512]{1,0:T(8,128)(2,1)S(1)} %collective-permute-done.18.refs_2_), channel_id=1, source_target_pairs={{0,1},{1,0},{2,3},{3,2},{4,5},{5,4},{6,7},{7,6},{8,9},{9,8},{10,11... | collective-permute-start | bytes 1376264 | tf_op jit(solution)/shard_map/ppermute | solution.py:32
  197.9 2.0 copy.23
  201.1 8.9 %final.1 = (bf16[512,896]{1,0:T(8,128)(2,1)}, bf16[512,896]{1,0:T(8,128)(2,1)}) custom-call(s32[8]{0:T(128)} %fusion.19.heads, bf16[448,512]{1,0:T(8,128)(2,1)} %get-tuple-element.49.refs_0_, bf16[448,512]{1,0:T(8,128)(2,1)} %copy-done.13, bf16[448,512]{1,0:T(8,128)(2,1)} %copy-done.10, bf16[448,512]{1,0:T(8,128)(2,1)} %copy-done.14, ...), custom_call_target="tpu_custom_call" | custom-call | flops 3288334336 | bytes 6000000 | tf_op jit(solution)/shard_map/final/pallas_call | solution.py:341
  (131 shorter events, 12.3 us)
Async XLA Ops:
  8.5 11.3 %copy-start.1 = (bf16[512,448]{0,1:T(8,128)(2,1)S(1)}, bf16[512,448]{0,1:T(8,128)(2,1)}, u32[]{:S(2)}) copy-start(bf16[512,448]{0,1:T(8,128)(2,1)} %param.20) | copy-start | bytes 1376260
  8.5 16.6 %copy-start.34 = (s32[8]{0:T(128)S(1)}, s32[8]{0:T(128)}, u32[]{:S(2)}) copy-start(s32[8]{0:T(128)} %constant.200) | copy-start | bytes 100
  8.5 46.9 %copy-start.32 = (s32[1024]{0:T(1024)S(1)}, s32[1024]{0:T(1024)}, u32[]{:S(2)}) copy-start(s32[1024]{0:T(1024)} %param.18) | copy-start | bytes 12292
  8.7 54.2 %copy-start.4 = (bf16[512,1024]{1,0:T(8,128)(2,1)}, bf16[512,1024]{1,0:T(8,128)(2,1)S(1)}, u32[]{:S(2)}) copy-start(bf16[512,1024]{1,0:T(8,128)(2,1)S(1)} %pad_maximum_fusion.refs_8_) | copy-start | bytes 3145732
  8.7 43.4 %collective-permute-start.3 = (bf16[512,1024]{1,0:T(8,128)(2,1)S(1)}, bf16[512,1024]{1,0:T(8,128)(2,1)}, u32[]{:S(2)}, u32[]{:S(2)}) collective-permute-start(bf16[512,1024]{1,0:T(8,128)(2,1)S(1)} %pad_maximum_fusion.refs_8_), channel_id=1, source_target_pairs={{0,64},{1,65},{2,66},{3,67},{4,68},{5,69},{6,70},{7,71},{8,72},{9,... | collective-permute-start | bytes 3145736 | tf_op jit(solution)/shard_map/ppermute | solution.py:32
  10.0 42.1 %collective-permute-start.4 = (bf16[512,1024]{1,0:T(8,128)(2,1)S(1)}, bf16[512,1024]{1,0:T(8,128)(2,1)}, u32[]{:S(2)}, u32[]{:S(2)}) collective-permute-start(bf16[512,1024]{1,0:T(8,128)(2,1)S(1)} %pad_maximum_fusion.refs_8_), channel_id=1, source_target_pairs={{0,192},{1,193},{2,194},{3,195},{4,196},{5,197},{6,198},{7,199},{8... | collective-permute-start | bytes 3145736 | tf_op jit(solution)/shard_map/ppermute | solution.py:32
  11.4 40.7 %collective-permute-start.9 = (bf16[512,1024]{1,0:T(8,128)(2,1)S(1)}, bf16[512,1024]{1,0:T(8,128)(2,1)S(1)}, u32[]{:S(2)}, u32[]{:S(2)}) collective-permute-start(bf16[512,1024]{1,0:T(8,128)(2,1)S(1)} %pad_maximum_fusion.refs_8_), channel_id=1, source_target_pairs={{0,1},{1,0},{2,3},{3,2},{4,5},{5,4},{6,7},{7,6},{8,9},{9,8},{10,11... | collective-permute-start | bytes 3145736 | tf_op jit(solution)/shard_map/ppermute | solution.py:32
  12.7 17.1 %collective-permute-start = (bf16[112,1024]{1,0:T(8,128)(2,1)S(1)}, bf16[112,1024]{1,0:T(8,128)(2,1)S(1)}, u32[]{:S(2)}, u32[]{:S(2)}) collective-permute-start(bf16[112,1024]{1,0:T(8,128)(2,1)S(1)} %pad_maximum_fusion.1), channel_id=1, source_target_pairs={{0,0},{1,32},{2,2},{3,34},{4,4},{5,36},{6,6},{7,38},{8,64},{9,96},... | collective-permute-start | bytes 688136 | tf_op jit(solution)/shard_map/ppermute | solution.py:44
  20.6 9.3 %all-to-all-start = ((f32[8,1,512]{2,1,0:T(1,128)}), f32[8,1,512]{2,1,0:T(1,128)S(1)}, u32[]{:S(2)}, u32[]{:S(2)}) async-start(f32[8,1,512]{2,1,0:T(1,128)} %broadcast_in_dim.84), calls=%async_computation | async-start | bytes 32768 | tf_op jit(solution)/shard_map/all_to_all | solution.py:188
  25.1 174.8 %all-gather.2.cloned.1.call-start = ((), (), s32[]{:S(2)}) async-start(), calls=%async_computation.5 | async-start | bytes 6623232 | tf_op jit(solution)/shard_map/all_gather | solution.py:278
  29.9 31.1 %copy-start.18 = (bf16[112,1024]{1,0:T(8,128)(2,1)}, bf16[112,1024]{1,0:T(8,128)(2,1)S(1)}, u32[]{:S(2)}) copy-start(bf16[112,1024]{1,0:T(8,128)(2,1)S(1)} %collective-permute-done.refs_0_) | copy-start | bytes 688132
  29.9 6.6 %collective-permute-start.1 = (bf16[112,1024]{1,0:T(8,128)(2,1)S(1)}, bf16[112,1024]{1,0:T(8,128)(2,1)S(1)}, u32[]{:S(2)}, u32[]{:S(2)}) collective-permute-start(bf16[112,1024]{1,0:T(8,128)(2,1)S(1)} %collective-permute-done.refs_0_), channel_id=1, source_target_pairs={{0,8},{1,9},{2,10},{3,11},{4,12},{5,13},{6,14},{7,15},{8,16},{9,17... | collective-permute-start | bytes 688136 | tf_op jit(solution)/shard_map/ppermute | solution.py:32
  31.7 8.2 %collective-permute-start.6 = (bf16[112,1024]{1,0:T(8,128)(2,1)S(1)}, bf16[112,1024]{1,0:T(8,128)(2,1)S(1)}, u32[]{:S(2)}, u32[]{:S(2)}) collective-permute-start(bf16[112,1024]{1,0:T(8,128)(2,1)S(1)} %collective-permute-done.refs_0_), channel_id=1, source_target_pairs={{0,56},{1,57},{2,58},{3,59},{4,60},{5,61},{6,62},{7,63},{8,0},{9,1... | collective-permute-start | bytes 688136 | tf_op jit(solution)/shard_map/ppermute | solution.py:32
  36.5 29.1 %copy-start.19 = (bf16[112,1024]{1,0:T(8,128)(2,1)}, bf16[112,1024]{1,0:T(8,128)(2,1)S(1)}, u32[]{:S(2)}) copy-start(bf16[112,1024]{1,0:T(8,128)(2,1)S(1)} %collective-permute-done.1.refs_1_) | copy-start | bytes 688132
  36.5 5.4 %collective-permute-start.2 = (bf16[112,1024]{1,0:T(8,128)(2,1)S(1)}, bf16[112,1024]{1,0:T(8,128)(2,1)S(1)}, u32[]{:S(2)}, u32[]{:S(2)}) collective-permute-start(bf16[112,1024]{1,0:T(8,128)(2,1)S(1)} %collective-permute-done.1.refs_1_), channel_id=1, source_target_pairs={{0,8},{1,9},{2,10},{3,11},{4,12},{5,13},{6,14},{7,15},{8,16},{9,17... | collective-permute-start | bytes 688136 | tf_op jit(solution)/shard_map/ppermute | solution.py:32
  40.0 12.2 %copy-start.20 = (bf16[112,1024]{1,0:T(8,128)(2,1)}, bf16[112,1024]{1,0:T(8,128)(2,1)S(1)}, u32[]{:S(2)}) copy-start(bf16[112,1024]{1,0:T(8,128)(2,1)S(1)} %collective-permute-done.6.refs_5_) | copy-start | bytes 688132
  40.0 6.5 %collective-permute-start.7 = (bf16[112,1024]{1,0:T(8,128)(2,1)S(1)}, bf16[112,1024]{1,0:T(8,128)(2,1)S(1)}, u32[]{:S(2)}, u32[]{:S(2)}) collective-permute-start(bf16[112,1024]{1,0:T(8,128)(2,1)S(1)} %collective-permute-done.6.refs_5_), channel_id=1, source_target_pairs={{0,56},{1,57},{2,58},{3,59},{4,60},{5,61},{6,62},{7,63},{8,0},{9,1... | collective-permute-start | bytes 688136 | tf_op jit(solution)/shard_map/ppermute | solution.py:32
  41.9 10.2 %copy-start.21 = (bf16[112,1024]{1,0:T(8,128)(2,1)}, bf16[112,1024]{1,0:T(8,128)(2,1)S(1)}, u32[]{:S(2)}) copy-start(bf16[112,1024]{1,0:T(8,128)(2,1)S(1)} %collective-permute-done.2.refs_2_) | copy-start | bytes 688132
  41.9 7.3 %collective-permute-start.5 = (bf16[112,1024]{1,0:T(8,128)(2,1)S(1)}, bf16[112,1024]{1,0:T(8,128)(2,1)}, u32[]{:S(2)}, u32[]{:S(2)}) collective-permute-start(bf16[112,1024]{1,0:T(8,128)(2,1)S(1)} %collective-permute-done.2.refs_2_), channel_id=1, source_target_pairs={{0,8},{1,9},{2,10},{3,11},{4,12},{5,13},{6,14},{7,15},{8,16},{9,17... | collective-permute-start | bytes 688136 | tf_op jit(solution)/shard_map/ppermute | solution.py:32
  46.4 5.7 %copy-start.22 = (bf16[112,1024]{1,0:T(8,128)(2,1)}, bf16[112,1024]{1,0:T(8,128)(2,1)S(1)}, u32[]{:S(2)}) copy-start(bf16[112,1024]{1,0:T(8,128)(2,1)S(1)} %collective-permute-done.7.refs_6_) | copy-start | bytes 688132
  46.4 5.7 %collective-permute-start.8 = (bf16[112,1024]{1,0:T(8,128)(2,1)S(1)}, bf16[112,1024]{1,0:T(8,128)(2,1)S(1)}, u32[]{:S(2)}, u32[]{:S(2)}) collective-permute-start(bf16[112,1024]{1,0:T(8,128)(2,1)S(1)} %collective-permute-done.7.refs_6_), channel_id=1, source_target_pairs={{0,56},{1,57},{2,58},{3,59},{4,60},{5,61},{6,62},{7,63},{8,0},{9,1... | collective-permute-start | bytes 688136 | tf_op jit(solution)/shard_map/ppermute | solution.py:32
  52.8 12.7 %collective-permute-start.11 = (bf16[512,1024]{1,0:T(8,128)(2,1)}, bf16[512,1024]{1,0:T(8,128)(2,1)}, u32[]{:S(2)}, u32[]{:S(2)}) collective-permute-start(bf16[512,1024]{1,0:T(8,128)(2,1)} %collective-permute-done.3.refs_9_), channel_id=1, source_target_pairs={{0,1},{1,0},{2,3},{3,2},{4,5},{5,4},{6,7},{7,6},{8,9},{9,8},{10,11... | collective-permute-start | bytes 3145736 | tf_op jit(solution)/shard_map/ppermute | solution.py:32
  55.3 10.2 %collective-permute-start.12 = (bf16[512,1024]{1,0:T(8,128)(2,1)}, bf16[512,1024]{1,0:T(8,128)(2,1)}, u32[]{:S(2)}, u32[]{:S(2)}) collective-permute-start(bf16[512,1024]{1,0:T(8,128)(2,1)} %collective-permute-done.4.refs_10_), channel_id=1, source_target_pairs={{0,1},{1,0},{2,3},{3,2},{4,5},{5,4},{6,7},{7,6},{8,9},{9,8},{10,11... | collective-permute-start | bytes 3145736 | tf_op jit(solution)/shard_map/ppermute | solution.py:32
  56.0 9.5 %collective-permute-start.10 = (bf16[112,1024]{1,0:T(8,128)(2,1)}, bf16[112,1024]{1,0:T(8,128)(2,1)S(1)}, u32[]{:S(2)}, u32[]{:S(2)}) collective-permute-start(bf16[112,1024]{1,0:T(8,128)(2,1)} %collective-permute-done.5.refs_3_), channel_id=1, source_target_pairs={{0,8},{1,9},{2,10},{3,11},{4,12},{5,13},{6,14},{7,15},{8,16},{9,17... | collective-permute-start | bytes 688136 | tf_op jit(solution)/shard_map/ppermute | solution.py:32
  62.8 15.7 %collective-permute-start.13 = (bf16[256,1024]{1,0:T(8,128)(2,1)S(1)}, bf16[256,1024]{1,0:T(8,128)(2,1)S(1)}, u32[]{:S(2)}, u32[]{:S(2)}) collective-permute-start(bf16[256,1024]{1,0:T(8,128)(2,1)S(1)} %slice.38), channel_id=1, source_target_pairs={{0,64},{1,65},{2,66},{3,67},{4,68},{5,69},{6,70},{7,71},{8,72},{9,... | collective-permute-start | bytes 1572872 | tf_op jit(solution)/shard_map/ppermute | solution.py:32
  62.8 17.8 %collective-permute-start.14 = (bf16[256,1024]{1,0:T(8,128)(2,1)}, bf16[256,1024]{1,0:T(8,128)(2,1)S(1)}, u32[]{:S(2)}, u32[]{:S(2)}) collective-permute-start(bf16[256,1024]{1,0:T(8,128)(2,1)} %slice.39), channel_id=1, source_target_pairs={{0,192},{1,193},{2,194},{3,195},{4,196},{5,197},{6,198},{7,199},{8... | collective-permute-start | bytes 1572872 | tf_op jit(solution)/shard_map/ppermute | solution.py:32
  74.0 21.0 %all-to-all-start.1 = ((bf16[4,112,1536]{2,1,0:T(8,128)(2,1)}), bf16[4,112,1536]{2,1,0:T(8,128)(2,1)S(1)}, u32[]{:S(2)}, u32[]{:S(2)}) async-start(bf16[4,112,1536]{2,1,0:T(8,128)(2,1)} %part.2), calls=%async_computation.1 | async-start | bytes 2752512 | tf_op jit(solution)/shard_map/all_to_all | solution.py:298
  78.3 10.5 %copy-start.28 = (s32[4]{0:T(128)}, s32[4]{0:T(128)S(1)}, u32[]{:S(2)}) copy-start(s32[4]{0:T(128)S(1)} %get-tuple-element.69.xs) | copy-start | bytes 52
  78.6 3.7 %collective-permute-start.15 = (bf16[256,1024]{1,0:T(8,128)(2,1)S(1)}, bf16[256,1024]{1,0:T(8,128)(2,1)S(1)}, u32[]{:S(2)}, u32[]{:S(2)}) collective-permute-start(bf16[256,1024]{1,0:T(8,128)(2,1)S(1)} %collective-permute-done.13.refs_8_), channel_id=1, source_target_pairs={{0,1},{1,0},{2,3},{3,2},{4,5},{5,4},{6,7},{7,6},{8,9},{9,8},{10,11... | collective-permute-start | bytes 1572872 | tf_op jit(solution)/shard_map/ppermute | solution.py:32
  80.7 2.4 %collective-permute-start.16 = (bf16[256,1024]{1,0:T(8,128)(2,1)S(1)}, bf16[256,1024]{1,0:T(8,128)(2,1)}, u32[]{:S(2)}, u32[]{:S(2)}) collective-permute-start(bf16[256,1024]{1,0:T(8,128)(2,1)S(1)} %collective-permute-done.14.refs_9_), channel_id=1, source_target_pairs={{0,1},{1,0},{2,3},{3,2},{4,5},{5,4},{6,7},{7,6},{8,9},{9,8},{10,11... | collective-permute-start | bytes 1572872 | tf_op jit(solution)/shard_map/ppermute | solution.py:32
  95.0 10.0 %copy-start = (bf16[4,112,1536]{2,1,0:T(8,128)(2,1)}, bf16[4,112,1536]{2,1,0:T(8,128)(2,1)S(1)}, u32[]{:S(2)}) copy-start(bf16[4,112,1536]{2,1,0:T(8,128)(2,1)S(1)} %all-to-all-done.1.first) | copy-start | bytes 4128772
  95.0 10.0 %all-to-all-start.2 = ((bf16[4,112,512]{2,1,0:T(8,128)(2,1)}), bf16[4,112,512]{2,1,0:T(8,128)(2,1)S(1)}, u32[]{:S(2)}, u32[]{:S(2)}) async-start(bf16[4,112,512]{2,1,0:T(8,128)(2,1)} %part.3), calls=%async_computation.2 | async-start | bytes 917504 | tf_op jit(solution)/shard_map/all_to_all | solution.py:298
  99.8 17.8 %copy-start.29 = (bf16[448]{0:T(512)(128)(2,1)S(1)}, bf16[448]{0:T(512)(128)(2,1)}, u32[]{:S(2)}) copy-start(bf16[448]{0:T(512)(128)(2,1)} %param.21) | copy-start | bytes 2692
  99.8 17.9 %copy-start.30 = (bf16[448]{0:T(512)(128)(2,1)S(1)}, bf16[448]{0:T(512)(128)(2,1)}, u32[]{:S(2)}) copy-start(bf16[448]{0:T(512)(128)(2,1)} %param.22) | copy-start | bytes 2692
  99.8 18.7 %copy-start.5 = (bf16[512,896]{1,0:T(8,128)(2,1)S(1)}, bf16[512,896]{1,0:T(8,128)(2,1)}, u32[]{:S(2)}) copy-start(bf16[512,896]{1,0:T(8,128)(2,1)} %param.23) | copy-start | bytes 2752516
  110.4 8.2 %copy-start.6 = (bf16[512,896]{1,0:T(8,128)(2,1)S(1)}, bf16[512,896]{1,0:T(8,128)(2,1)}, u32[]{:S(2)}) copy-start(bf16[512,896]{1,0:T(8,128)(2,1)} %param.24) | copy-start | bytes 2752516
  110.4 41.2 %all-to-all-start.3 = ((bf16[32,112,128]{2,1,0:T(8,128)(2,1)}), bf16[32,112,128]{2,1,0:T(8,128)(2,1)S(1)}, u32[]{:S(2)}, u32[]{:S(2)}) async-start(bf16[32,112,128]{2,1,0:T(8,128)(2,1)} %send.1), calls=%async_computation.3 | async-start | bytes 1835008 | tf_op jit(solution)/shard_map/all_to_all | solution.py:314
  121.8 34.3 %copy-start.27 = (f32[512]{0:T(512)}, f32[512]{0:T(512)S(1)}, u32[]{:S(2)}) copy-start(f32[512]{0:T(512)S(1)} %add_rsqrt_fusion) | copy-start | bytes 6148
  156.1 12.7 %all-to-all-start.4 = ((f32[8,4,512]{2,1,0:T(4,128)}), f32[8,4,512]{2,1,0:T(4,128)S(1)}, u32[]{:S(2)}, u32[]{:S(2)}) async-start(f32[8,4,512]{2,1,0:T(4,128)} %get-tuple-element.47), calls=%async_computation.4 | async-start | bytes 131072 | tf_op jit(solution)/shard_map/all_to_all | solution.py:326
  165.0 32.3 %copy-start.31 = (s32[8]{0:T(128)S(1)}, s32[8]{0:T(128)}, u32[]{:S(2)}) copy-start(s32[8]{0:T(128)} %constant.196.clone) | copy-start | bytes 100
  172.5 13.3 %collective-permute-start.18 = (bf16[448,512]{1,0:T(8,128)(2,1)}, bf16[448,512]{1,0:T(8,128)(2,1)S(1)}, u32[]{:S(2)}, u32[]{:S(2)}) collective-permute-start(bf16[448,512]{1,0:T(8,128)(2,1)} %get-tuple-element.49.refs_0_), channel_id=1, source_target_pairs={{0,2},{1,3},{2,4},{3,5},{4,6},{5,7},{6,0},{7,1},{8,10},{9,11},{10,... | collective-permute-start | bytes 1376264 | tf_op jit(solution)/shard_map/ppermute | solution.py:32
  172.8 23.9 %collective-permute-start.20 = (bf16[448,512]{1,0:T(8,128)(2,1)}, bf16[448,512]{1,0:T(8,128)(2,1)S(1)}, u32[]{:S(2)}, u32[]{:S(2)}) collective-permute-start(bf16[448,512]{1,0:T(8,128)(2,1)} %get-tuple-element.49.refs_0_), channel_id=1, source_target_pairs={{0,6},{1,7},{2,0},{3,1},{4,2},{5,3},{6,4},{7,5},{8,14},{9,15},{10,... | collective-permute-start | bytes 1376264 | tf_op jit(solution)/shard_map/ppermute | solution.py:32
  175.2 21.6 %collective-permute-start.22 = (bf16[448,512]{1,0:T(8,128)(2,1)}, bf16[448,512]{1,0:T(8,128)(2,1)S(1)}, u32[]{:S(2)}, u32[]{:S(2)}) collective-permute-start(bf16[448,512]{1,0:T(8,128)(2,1)} %get-tuple-element.49.refs_0_), channel_id=1, source_target_pairs={{0,4},{1,5},{2,6},{3,7},{4,0},{5,1},{6,2},{7,3},{8,12},{9,13},{10,... | collective-permute-start | bytes 1376264 | tf_op jit(solution)/shard_map/ppermute | solution.py:32
  175.2 24.7 %collective-permute-start.17 = (bf16[448,512]{1,0:T(8,128)(2,1)}, bf16[448,512]{1,0:T(8,128)(2,1)S(1)}, u32[]{:S(2)}, u32[]{:S(2)}) collective-permute-start(bf16[448,512]{1,0:T(8,128)(2,1)} %get-tuple-element.49.refs_0_), channel_id=1, source_target_pairs={{0,1},{1,0},{2,3},{3,2},{4,5},{5,4},{6,7},{7,6},{8,9},{9,8},{10,11... | collective-permute-start | bytes 1376264 | tf_op jit(solution)/shard_map/ppermute | solution.py:32
  185.8 14.2 %copy-start.10 = (bf16[448,512]{1,0:T(8,128)(2,1)}, bf16[448,512]{1,0:T(8,128)(2,1)S(1)}, u32[]{:S(2)}) copy-start(bf16[448,512]{1,0:T(8,128)(2,1)S(1)} %collective-permute-done.18.refs_2_) | copy-start | bytes 1376260
  185.8 14.1 %collective-permute-start.19 = (bf16[448,512]{1,0:T(8,128)(2,1)S(1)}, bf16[448,512]{1,0:T(8,128)(2,1)S(1)}, u32[]{:S(2)}, u32[]{:S(2)}) collective-permute-start(bf16[448,512]{1,0:T(8,128)(2,1)S(1)} %collective-permute-done.18.refs_2_), channel_id=1, source_target_pairs={{0,1},{1,0},{2,3},{3,2},{4,5},{5,4},{6,7},{7,6},{8,9},{9,8},{10,11... | collective-permute-start | bytes 1376264 | tf_op jit(solution)/shard_map/ppermute | solution.py:32
  196.7 3.2 %collective-permute-start.21 = (bf16[448,512]{1,0:T(8,128)(2,1)S(1)}, bf16[448,512]{1,0:T(8,128)(2,1)S(1)}, u32[]{:S(2)}, u32[]{:S(2)}) collective-permute-start(bf16[448,512]{1,0:T(8,128)(2,1)S(1)} %collective-permute-done.20.refs_4_), channel_id=1, source_target_pairs={{0,1},{1,0},{2,3},{3,2},{4,5},{5,4},{6,7},{7,6},{8,9},{9,8},{10,11... | collective-permute-start | bytes 1376264 | tf_op jit(solution)/shard_map/ppermute | solution.py:32
  196.8 3.2 %collective-permute-start.23 = (bf16[448,512]{1,0:T(8,128)(2,1)S(1)}, bf16[448,512]{1,0:T(8,128)(2,1)S(1)}, u32[]{:S(2)}, u32[]{:S(2)}) collective-permute-start(bf16[448,512]{1,0:T(8,128)(2,1)S(1)} %collective-permute-done.22.refs_6_), channel_id=1, source_target_pairs={{0,1},{1,0},{2,3},{3,2},{4,5},{5,4},{6,7},{7,6},{8,9},{9,8},{10,11... | collective-permute-start | bytes 1376264 | tf_op jit(solution)/shard_map/ppermute | solution.py:32
  (17 other events, 35.7 us)
Sparse Core Ops, SparseCore 0:
  52.9 109.1 all-gather.1
